TPU v7x, 32 devices: a whole 2x2x4 slice. The times are simulated.
32 devices in a mesh: groups: 2 (over x), space: 16 (over z, y, core).
Axes of the slice: x: 2, y: 2, z: 4, core: 2. Of those that a mesh axis runs over, the one named last changes fastest.
Arguments:
- grid_in: bfloat16 [96, 1440, 128], P(('groups', 'space')), parts along dimension 0, may hold values from -6 to 6
- upstream: bfloat16 [96, 1440, 128], P(('groups', 'space')), parts along dimension 0, may hold values from -6 to 6
- mix_weight: bfloat16 [2, 128, 128], replicated, may hold values from -0.375 to 0.375
- degree_filter: bfloat16 [512, 128], replicated, may hold values from 0.25 to 2
Outputs:
- grad_in: bfloat16 [96, 1440, 128], P(('groups', 'space')), parts along dimension 0
- grad_weight: float32 [4, 128, 128], P('groups'), parts along dimension 0
- grad_filter: float32 [1024, 128], P('groups'), parts along dimension 0
There are 2 independent parts, one for each index of `groups`. A program takes and returns all parts, laid end to end along the dimension named above; an argument that names none is the same for every part. Nothing has to cross between parts.
All inputs are finite; a program needn't handle non-finite values.
Results may differ from a plain program's by a relative error of at most 0.02.
Values may be sent and summed in bfloat16 or wider, within the bound.
No kernel may reach another device: no remote copies, remote signals or barrier semaphores. Data moves between devices by JAX's collectives and lax.ppermute only.
A program may use at most 128 MiB of HBM per device.

v0:
```python
import math

import jax
import jax.numpy as jnp
from jax import lax
from jax.sharding import PartitionSpec as P

MODES = 512


def latitude_angles(lat_count):
    lat_index = jnp.arange(lat_count, dtype=jnp.float32)
    return math.pi * (lat_index + 0.5) / lat_count


def latitude_weights(lat_count):
    return math.pi / lat_count * jnp.sin(latitude_angles(lat_count))


def legendre_rows(m_values, lat_count, mode_count):
    angles = latitude_angles(lat_count)
    cosine = jnp.cos(angles)[None, :]
    sine_lat = jnp.sin(angles)[None, :]
    orders = m_values.astype(jnp.float32)[:, None]
    log_start = 0.5 * (jnp.log(2.0 * orders + 1.0) - math.log(2.0))
    log_start = log_start + 0.5 * (
        lax.lgamma(2.0 * orders + 1.0) - 2.0 * lax.lgamma(orders + 1.0) - orders * math.log(4.0)
    )
    log_start = log_start + orders * jnp.log(sine_lat)

    def degree_block(carry, block_index):
        p_now, p_prev, log_scale = carry
        outputs = []
        for inner_step in range(32):
            degree = (block_index * 32 + inner_step).astype(jnp.float32)
            active = degree > orders
            denom = jnp.maximum(degree * degree - orders * orders, 1.0)
            coef_a = jnp.sqrt((4.0 * degree * degree - 1.0) / denom)
            lower = jnp.maximum((degree - 1.0) * (degree - 1.0) - orders * orders, 0.0)
            coef_b = jnp.sqrt(
                lower * (2.0 * degree + 1.0) / (jnp.maximum(2.0 * degree - 3.0, 1.0) * denom)
            )
            p_next = jnp.where(active, coef_a * cosine * p_now - coef_b * p_prev, p_now)
            p_prev = jnp.where(active, p_now, p_prev)
            p_now = p_next
            outputs.append(jnp.where(degree >= orders, p_now * jnp.exp(log_scale), 0.0))
        magnitude = jnp.maximum(jnp.abs(p_now), jnp.abs(p_prev))
        next_carry = (p_now / magnitude, p_prev / magnitude, log_scale + jnp.log(magnitude))
        return (next_carry, jnp.stack(outputs, 1))

    ones_grid = jnp.ones((m_values.shape[0], lat_count), jnp.float32)
    start_carry = (ones_grid, jnp.zeros_like(ones_grid), log_start * ones_grid)
    block_ids = jnp.arange(mode_count // 32, dtype=jnp.int32)
    final_carry, stacked = lax.scan(degree_block, start_carry, block_ids)
    return jnp.transpose(stacked, (1, 0, 2, 3)).reshape(m_values.shape[0], mode_count, lat_count)


def fourier_tables(m_order, lon_count):
    lon_index = jnp.arange(lon_count, dtype=jnp.int32)
    phases = m_order[:, None] * lon_index[None, :] % lon_count
    angles = 2.0 * math.pi / lon_count * phases.astype(jnp.float32)
    factor = 1.0 / math.sqrt(lon_count)
    analysis = jnp.stack([jnp.cos(angles) * factor, -jnp.sin(angles) * factor], 1)
    analysis = analysis.reshape(2 * m_order.shape[0], lon_count).astype(jnp.bfloat16)
    doubling = jnp.where(m_order == 0, 1.0, 2.0).astype(jnp.bfloat16)
    synthesis = analysis * jnp.repeat(doubling, 2)[:, None]
    return (analysis, synthesis)


def mixing_matrix(mix_weight):
    upper = jnp.concatenate([mix_weight[0], mix_weight[1]], 1)
    lower = jnp.concatenate([-mix_weight[1], mix_weight[0]], 1)
    return jnp.concatenate([upper, lower], 0)


def fold_weight(block_grad):
    half = block_grad.shape[0] // 2
    real_part = block_grad[:half, :half] + block_grad[half:, half:]
    imag_part = block_grad[:half, half:] - block_grad[half:, :half]
    return jnp.stack([real_part, imag_part], 0)


def gelu_slope(field):
    return 0.5 * (1.0 + lax.erf(field * (1.0 / math.sqrt(2.0)))) + field * jnp.exp(
        -0.5 * field * field
    ) * (1.0 / math.sqrt(2.0 * math.pi))


def body(grid_in, upstream, mix_weight, degree_filter):
    devices = lax.axis_size("space")
    device_index = lax.axis_index("space")
    lat_local, lon_count, channels = grid_in.shape
    lat_count = lat_local * devices
    per_device = MODES // devices
    positions = jnp.arange(MODES, dtype=jnp.int32)
    slot_index = jnp.arange(per_device, dtype=jnp.int32)
    m_order = positions % per_device * devices + positions // per_device
    slot_orders = slot_index * devices + device_index
    quarter = per_device // 4
    sections = [
        (part_id * quarter, (part_id + 1) * quarter, part_id * (MODES // 4)) for part_id in range(4)
    ]
    analysis, synthesis = fourier_tables(m_order, lon_count)
    legendre = legendre_rows(slot_orders, lat_count, MODES)
    synth_table = legendre.astype(jnp.bfloat16)
    anal_table = (legendre * latitude_weights(lat_count)).astype(jnp.bfloat16)
    wide_weight = mixing_matrix(mix_weight)
    filter_gain = degree_filter.astype(jnp.float32)
    fourier = jnp.einsum("kn,anc->akc", analysis, grid_in, preferred_element_type=jnp.float32)
    fourier = fourier.astype(jnp.bfloat16).reshape(lat_local, MODES, 2 * channels)
    spectral_in = lax.all_to_all(fourier, "space", split_axis=1, concat_axis=0, tiled=True)
    saved = []
    pieces = []
    for start_slot, stop_slot, first_degree in sections:
        spectrum = jnp.einsum(
            "jla,ajx->jlx",
            anal_table[start_slot:stop_slot, first_degree:],
            spectral_in[:, start_slot:stop_slot],
            preferred_element_type=jnp.float32,
        ).astype(jnp.bfloat16)
        slot_count, degree_count = (spectrum.shape[0], spectrum.shape[1])
        spectrum = spectrum.reshape(slot_count, degree_count, 2, channels)
        scaled = (
            spectrum.astype(jnp.float32) * filter_gain[first_degree:][None, :, None, :]
        ).astype(jnp.bfloat16)
        scaled_rows = scaled.reshape(slot_count * degree_count, 2 * channels)
        mixed = jnp.dot(scaled_rows, wide_weight, preferred_element_type=jnp.float32).astype(
            jnp.bfloat16
        )
        mixed = mixed.reshape(slot_count, degree_count, 2 * channels)
        pieces.append(
            jnp.einsum(
                "jla,jlx->ajx",
                synth_table[start_slot:stop_slot, first_degree:],
                mixed,
                preferred_element_type=jnp.float32,
            ).astype(jnp.bfloat16)
        )
        saved.append((spectrum, scaled_rows))
    grid_modes = jnp.concatenate(pieces, 1)
    returned = lax.all_to_all(grid_modes, "space", split_axis=0, concat_axis=1, tiled=True)
    field = jnp.einsum(
        "kn,akc->anc",
        synthesis,
        returned.reshape(lat_local, 2 * MODES, channels),
        preferred_element_type=jnp.float32,
    )
    slope = (upstream.astype(jnp.float32) * gelu_slope(field)).astype(jnp.bfloat16)
    gfourier = jnp.einsum("kn,anc->akc", synthesis, slope, preferred_element_type=jnp.float32)
    gfourier = gfourier.astype(jnp.bfloat16).reshape(lat_local, MODES, 2 * channels)
    gradient_in = lax.all_to_all(gfourier, "space", split_axis=1, concat_axis=0, tiled=True)
    weight_total = jnp.zeros((2 * channels, 2 * channels), jnp.float32)
    filter_total = jnp.zeros((MODES, channels), jnp.float32)
    gpieces = []
    for (start_slot, stop_slot, first_degree), (spectrum, scaled_rows) in zip(sections, saved):
        gmixed = jnp.einsum(
            "jla,ajx->jlx",
            synth_table[start_slot:stop_slot, first_degree:],
            gradient_in[:, start_slot:stop_slot],
            preferred_element_type=jnp.float32,
        ).astype(jnp.bfloat16)
        slot_count, degree_count = (gmixed.shape[0], gmixed.shape[1])
        gmixed_rows = gmixed.reshape(slot_count * degree_count, 2 * channels)
        weight_total = weight_total + lax.dot_general(
            scaled_rows, gmixed_rows, (((0,), (0,)), ((), ())), preferred_element_type=jnp.float32
        )
        gscaled = lax.dot_general(
            gmixed_rows, wide_weight, (((1,), (1,)), ((), ())), preferred_element_type=jnp.float32
        )
        gscaled = gscaled.reshape(slot_count, degree_count, 2, channels)
        filter_part = jnp.sum(gscaled * spectrum.astype(jnp.float32), axis=(0, 2))
        filter_total = filter_total + jnp.pad(filter_part, ((first_degree, 0), (0, 0)))
        gspectrum = (gscaled * filter_gain[first_degree:][None, :, None, :]).astype(jnp.bfloat16)
        gspectrum = gspectrum.reshape(slot_count, degree_count, 2 * channels)
        gpieces.append(
            jnp.einsum(
                "jla,jlx->ajx",
                anal_table[start_slot:stop_slot, first_degree:],
                gspectrum,
                preferred_element_type=jnp.float32,
            ).astype(jnp.bfloat16)
        )
    gfield_modes = jnp.concatenate(gpieces, 1)
    gfield = lax.all_to_all(gfield_modes, "space", split_axis=0, concat_axis=1, tiled=True)
    grad_in = jnp.einsum(
        "kn,akc->anc",
        analysis,
        gfield.reshape(lat_local, 2 * MODES, channels),
        preferred_element_type=jnp.float32,
    )
    grad_in = (grad_in + upstream.astype(jnp.float32)).astype(jnp.bfloat16)
    summed, grad_filter = lax.psum((weight_total * (1.0 / MODES), filter_total * 0.125), "space")
    grad_weight = fold_weight(summed)
    return (grad_in, grad_weight, grad_filter)


def solution(mesh):
    return jax.shard_map(
        body,
        mesh=mesh,
        in_specs=(P(("groups", "space"), None, None), P(("groups", "space"), None, None), P(), P()),
        out_specs=(P(("groups", "space"), None, None), P("groups", None, None), P("groups", None)),
        check_vma=False,
    )
```

profile of v0, /device:TPU:0, one launch (start us, length us, event | category | flops | bytes accessed | tf_op | source)
XLA Modules:
  0.0 464.1 jit_solution(1075074810099635511)
XLA Ops:
  7.2 12.8 %cosine_multiply_fusion = (bf16[512,1,1440]{0,2,1:T(8,128)(2,1)S(1)}, bf16[512,1,1440]{0,2,1:T(8,128)(2,1)S(1)}) fusion(s32[512]{0:T(512)S(1)} %fusion.108), kind=kLoop, calls=%fused_computation.328 | loop fusion | flops 10321920 | bytes 2951168 | tf_op jit(solution)/shard_map/mul | solution.py:63
  20.0 2.9 broadcast_multiply_fusion
  22.9 8.8 %copy.176 = bf16[512,2,1440]{2,1,0:T(2,128)(2,1)} copy(bf16[512,2,1440]{0,2,1:T(8,128)(2,1)} %get-tuple-element.620) | data formatting | bytes 5898240 | tf_op jit(solution)/shard_map/convert_element_type | solution.py:64
  31.8 7.5 %convert_element_type.660 = bf16[1024,1440]{1,0:T(8,128)(2,1)} reshape(bf16[512,2,1440]{2,1,0:T(2,128)(2,1)} %copy.176) | data formatting | bytes 5898240 | tf_op jit(solution)/shard_map/convert_element_type | solution.py:64
  39.3 3.7 fusion.54
  44.9 7.7 %all-to-all-start = ((bf16[3,512,256]{2,0,1:T(4,128)(2,1)}), bf16[3,512,256]{2,0,1:T(4,128)(2,1)}, u32[]{:S(2)}, u32[]{:S(2)}) async-start(bf16[3,512,256]{2,0,1:T(4,128)(2,1)} %copy.178), calls=%async_computation | async-start | bytes 2097152 | tf_op jit(solution)/shard_map/all_to_all | solution.py:111
  52.8 118.9 %while.23 = (s32[]{:T(128)}, f32[32,48]{1,0:T(8,128)S(1)}, f32[32,48]{1,0:T(8,128)S(1)}, f32[32,48]{1,0:T(8,128)S(1)}, f32[16,32,32,48]{3,1,2,0:T(8,128)}, /*ind...) while((s32[]{:T(128)}, f32[32,48]{1,0:T(8,128)S(1)}, ...), condition=%wide.region_1.2_spmd.clone.clone.clone.clone, body=%wide.region_0.1_spmd.clone.clone.clone.clone.sunk | while | flops 476130 | bytes 4452125 | solution.py:54
  173.8 5.2 %copy.242 = f32[32,512,48]{1,2,0:T(8,128)S(1)} copy(f32[32,512,48]{2,0,1:T(8,128)} %bitcast.851) | data formatting | bytes 6291456 | tf_op jit(solution)/shard_map/reshape | solution.py:55
  179.5 5.8 %copy.267 = f32[32,8,8,512]{3,1,2,0:T(8,128)} copy(f32[32,8,8,512]{3,2,1,0:T(8,128)S(1)} %bitcast.843) | data formatting | bytes 8388608
  196.9 2.3 fusion.127
  201.6 2.8 convert_convert_fusion
  204.4 5.8 %copy.184 = f32[4096,256]{0,1:T(8,128)} copy(f32[4096,256]{1,0:T(8,128)} %bitcast.841) | data formatting | bytes 8388608 | tf_op jit(solution)/shard_map/convert_element_type | solution.py:124
  211.9 2.4 copy.188
  214.3 5.0 %convolution_convert_fusion = bf16[4096,256]{1,0:T(8,128)(2,1)S(1)} fusion(f32[4096,256]{0,1:T(8,128)} %copy.184, f32[4096,256]{0,1:T(8,128)} %bitcast.842, bf16[128,128]{1,0:T(8,128)(2,1)S(1)} %get-tuple-element.776, bf16[128,128]{1,0:T(8,128)(2,1)S(1)} %fusion.126, bf16[128,128]{1,0:T(8,128)(2,1)S(1)} %get-tuple-element.775), kind=kOutput, calls=%fused_computation.300 | convolution fusion | flops 540540928 | bytes 10584064 | tf_op jit(solution)/shard_map/dot_general | solution.py:127
  224.5 2.8 fusion.47
  227.3 2.9 copy.192
  230.2 3.0 convolution_convert_fusion.2
  237.3 2.5 copy.196
  245.0 6.6 %all-to-all-start.1 = ((bf16[48,32,256]{2,1,0:T(8,128)(2,1)}), bf16[48,32,256]{2,1,0:T(8,128)(2,1)}, u32[]{:S(2)}, u32[]{:S(2)}) async-start(bf16[48,32,256]{2,1,0:T(8,128)(2,1)} %copy.197), calls=%async_computation.1 | async-start | bytes 1572864 | tf_op jit(solution)/shard_map/all_to_all | solution.py:141
  251.6 8.8 %copy.199 = bf16[512,2,1440]{2,1,0:T(2,128)(2,1)} copy(bf16[512,2,1440]{0,2,1:T(8,128)(2,1)} %get-tuple-element.619) | data formatting | bytes 5898240 | tf_op jit(solution)/shard_map/mul | solution.py:66
  260.4 7.5 %mul.4643 = bf16[1024,1440]{1,0:T(8,128)(2,1)} reshape(bf16[512,2,1440]{2,1,0:T(2,128)(2,1)} %copy.199) | data formatting | bytes 5898240 | tf_op jit(solution)/shard_map/mul | solution.py:66
  274.6 8.0 %fusion.57 = bf16[3,1024,128]{1,2,0:T(8,128)(2,1)} fusion(bf16[1024,1440]{1,0:T(8,128)(2,1)} %convert_element_type.660, bf16[1024]{0:T(1024)(128)(2,1)S(1)} %mul.4655, bf16[3,1440,128]{2,1,0:T(8,128)(2,1)} %param.7, bf16[3,1024,128]{2,1,0:T(8,128)(2,1)} %reshape.2792, bf16[1024,1440]{1,0:T(8,128)(2,1)} %mul.4643), kind=kOutput, calls=%fused_computation.363 | convolution fusion | flops 2272874496 | bytes 8579072 | tf_op jit(solution)/shard_map/kn,anc->akc/dot_general | solution.py:149
  282.5 2.3 copy.202
  286.9 2.8 copy.203
  289.7 5.5 %all-to-all-start.2 = ((bf16[3,512,256]{2,0,1:T(4,128)(2,1)}), bf16[3,512,256]{2,0,1:T(4,128)(2,1)}, u32[]{:S(2)}, u32[]{:S(2)}) async-start(bf16[3,512,256]{2,0,1:T(4,128)(2,1)} %copy.203), calls=%async_computation.2 | async-start | bytes 2097152 | tf_op jit(solution)/shard_map/all_to_all | solution.py:151
  296.1 5.3 %copy.247 = f32[8,512,256]{1,2,0:T(8,128)} copy(f32[8,512,256]{2,1,0:T(8,128)} %convert_convert_fusion) | data formatting | bytes 8388608 | tf_op jit(solution)/shard_map/convert_element_type | solution.py:124
  301.5 2.4 copy.248
  307.3 10.9 %all-to-all-done.2 = bf16[3,512,256]{2,0,1:T(4,128)(2,1)} async-done(((bf16[3,512,256]{2,0,1:T(4,128)(2,1)}), bf16[3,512,256]{2,0,1:T(4,128)(2,1)}, u32[]{:S(2)}, u32[]{:S(2)}) %all-to-all-start.2) | async-done | bytes 786464 | tf_op jit(solution)/shard_map/all_to_all | solution.py:151
  341.8 6.9 %all-to-all-start.3 = ((bf16[48,32,256]{2,1,0:T(8,128)(2,1)}), bf16[48,32,256]{2,1,0:T(8,128)(2,1)}, u32[]{:S(2)}, u32[]{:S(2)}) async-start(bf16[48,32,256]{2,1,0:T(8,128)(2,1)} %copy.214), calls=%async_computation.3 | async-start | bytes 1572864 | tf_op jit(solution)/shard_map/all_to_all | solution.py:184
  349.1 2.4 fusion.130
  355.1 92.1 %all-reduce.6.cloned.1.call-done = (f32[256,256]{1,0:T(8,128)}, f32[512,128]{0,1:T(8,128)}) async-done(((f32[256,256]{1,0:T(8,128)}, f32[512,128]{0,1:T(8,128)}), (f32[256,256]{1,0:T(8,128)}, f32[512,128]{0,1:T(8,128)})) %all-reduce.6.cloned.1.call-update) | async-done | bytes 524304 | tf_op jit(solution)/shard_map/psum | solution.py:192
  452.2 4.8 %fusion.31 = bf16[3,1440,128]{2,1,0:T(8,128)(2,1)} fusion(bf16[3,1024,128]{2,1,0:T(8,128)(2,1)S(1)} %reshape.2798, bf16[1024,1440]{1,0:T(8,128)(2,1)} %convert_element_type.660, bf16[3,1440,128]{2,1,0:T(8,128)(2,1)S(1)} %copy-done.35), kind=kOutput, calls=%fused_computation.333 | convolution fusion | flops 1134120960 | bytes 5947392 | tf_op jit(solution)/shard_map/kn,akc->anc/dot_general | solution.py:185
  (1775 shorter events, 169.3 us)
Async XLA Ops:
  7.2 32.1 %copy-start = (bf16[3,1440,128]{2,1,0:T(8,128)(2,1)S(1)}, bf16[3,1440,128]{2,1,0:T(8,128)(2,1)}, u32[]{:S(2)}) copy-start(bf16[3,1440,128]{2,1,0:T(8,128)(2,1)} %param.6) | copy-start | bytes 3317764
  44.9 154.4 %all-to-all-start = ((bf16[3,512,256]{2,0,1:T(4,128)(2,1)}), bf16[3,512,256]{2,0,1:T(4,128)(2,1)}, u32[]{:S(2)}, u32[]{:S(2)}) async-start(bf16[3,512,256]{2,0,1:T(4,128)(2,1)} %copy.178), calls=%async_computation | async-start | bytes 2097152 | tf_op jit(solution)/shard_map/all_to_all | solution.py:111
  52.8 118.9 %copy-start.20 = (bf16[512,128]{1,0:T(8,128)(2,1)S(1)}, bf16[512,128]{1,0:T(8,128)(2,1)}, u32[]{:S(2)}) copy-start(bf16[512,128]{1,0:T(8,128)(2,1)} %param.9) | copy-start | bytes 393220
  191.4 2.3 copy-start.25
  196.1 44.7 %copy-start.22 = (bf16[128,128]{1,0:T(8,128)(2,1)}, bf16[128,128]{1,0:T(8,128)(2,1)S(1)}, u32[]{:S(2)}) copy-start(bf16[128,128]{1,0:T(8,128)(2,1)S(1)} %fusion.126) | copy-start | bytes 98308
  196.9 44.0 %copy-start.23 = (bf16[128,128]{1,0:T(8,128)(2,1)}, bf16[128,128]{1,0:T(8,128)(2,1)S(1)}, u32[]{:S(2)}) copy-start(bf16[128,128]{1,0:T(8,128)(2,1)S(1)} %get-tuple-element.775) | copy-start | bytes 98308
  196.9 44.0 %copy-start.24 = (bf16[128,128]{1,0:T(8,128)(2,1)}, bf16[128,128]{1,0:T(8,128)(2,1)S(1)}, u32[]{:S(2)}) copy-start(bf16[128,128]{1,0:T(8,128)(2,1)S(1)} %get-tuple-element.776) | copy-start | bytes 98308
  199.3 2.4 copy-start.13
  214.3 7.1 %copy-start.6 = (f32[32,8,8,384]{3,1,2,0:T(8,128)S(1)}, f32[32,8,8,384]{3,1,2,0:T(8,128)}, u32[]{:S(2)}) copy-start(f32[32,8,8,384]{3,1,2,0:T(8,128)} %copy.268) | copy-start | bytes 9437188
  214.3 7.1 %copy-start.7 = (f32[3072,256]{0,1:T(8,128)S(1)}, f32[3072,256]{0,1:T(8,128)}, u32[]{:S(2)}) copy-start(f32[3072,256]{0,1:T(8,128)} %copy.188) | copy-start | bytes 9437188
  222.4 2.1 copy-start.28
  230.2 4.9 %copy-start.29 = (bf16[48,8,256]{2,1,0:T(8,128)(2,1)S(1)}, bf16[48,8,256]{2,1,0:T(8,128)(2,1)}, u32[]{:S(2)}) copy-start(bf16[48,8,256]{2,1,0:T(8,128)(2,1)} %get-tuple-element.768) | copy-start | bytes 589828
  239.9 3.9 copy-start.30
  239.9 3.9 copy-start.31
  239.9 3.9 copy-start.32
  245.0 25.4 %all-to-all-start.1 = ((bf16[48,32,256]{2,1,0:T(8,128)(2,1)}), bf16[48,32,256]{2,1,0:T(8,128)(2,1)}, u32[]{:S(2)}, u32[]{:S(2)}) async-start(bf16[48,32,256]{2,1,0:T(8,128)(2,1)} %copy.197), calls=%async_computation.1 | async-start | bytes 1572864 | tf_op jit(solution)/shard_map/all_to_all | solution.py:141
  289.7 28.5 %all-to-all-start.2 = ((bf16[3,512,256]{2,0,1:T(4,128)(2,1)}), bf16[3,512,256]{2,0,1:T(4,128)(2,1)}, u32[]{:S(2)}, u32[]{:S(2)}) async-start(bf16[3,512,256]{2,0,1:T(4,128)(2,1)} %copy.203), calls=%async_computation.2 | async-start | bytes 2097152 | tf_op jit(solution)/shard_map/all_to_all | solution.py:151
  303.8 2.2 copy-start.8
  320.7 3.7 copy-start.2
  321.4 8.7 %copy-start.4 = (bf16[8,384,256]{2,1,0:T(8,128)(2,1)}, bf16[8,384,256]{2,1,0:T(8,128)(2,1)S(1)}, u32[]{:S(2)}) copy-start(bf16[8,384,256]{2,1,0:T(8,128)(2,1)S(1)} %convolution_convert_fusion.4) | copy-start | bytes 4718596
  322.2 14.7 %copy-start.16 = (bf16[8,128,256]{2,1,0:T(8,128)(2,1)}, bf16[8,128,256]{2,1,0:T(8,128)(2,1)S(1)}, u32[]{:S(2)}) copy-start(bf16[8,128,256]{2,1,0:T(8,128)(2,1)S(1)} %convolution_convert_fusion.9) | copy-start | bytes 1572868
  327.8 2.3 copy-start.3
  327.8 2.3 copy-start.21
  340.6 8.4 %copy-start.10 = (bf16[32,8,8,512]{3,1,2,0:T(8,128)(2,1)S(1)}, bf16[32,8,8,512]{3,1,2,0:T(8,128)(2,1)}, u32[]{:S(2)}) copy-start(bf16[32,8,8,512]{3,1,2,0:T(8,128)(2,1)} %copy.271) | copy-start | bytes 6291460
  341.8 108.9 %all-to-all-start.3 = ((bf16[48,32,256]{2,1,0:T(8,128)(2,1)}), bf16[48,32,256]{2,1,0:T(8,128)(2,1)}, u32[]{:S(2)}, u32[]{:S(2)}) async-start(bf16[48,32,256]{2,1,0:T(8,128)(2,1)} %copy.214), calls=%async_computation.3 | async-start | bytes 1572864 | tf_op jit(solution)/shard_map/all_to_all | solution.py:184
  348.7 98.5 %all-reduce.6.cloned.1.call-start = ((), (), s32[]{:S(2)}) async-start(), calls=%async_computation.4 | async-start | bytes 1048576 | tf_op jit(solution)/shard_map/psum | solution.py:192
  349.0 2.5 copy-start.27
  349.0 2.5 copy-start.34
  349.0 3.3 copy-start.5
  349.1 3.3 copy-start.12
  447.3 5.0 %copy-start.35 = (bf16[3,1440,128]{2,1,0:T(8,128)(2,1)S(1)}, bf16[3,1440,128]{2,1,0:T(8,128)(2,1)}, u32[]{:S(2)}) copy-start(bf16[3,1440,128]{2,1,0:T(8,128)(2,1)} %param.7) | copy-start | bytes 3317764
  452.2 4.8 %copy-start.1 = (bf16[3,1440,128]{2,1,0:T(8,128)(2,1)S(1)}, bf16[3,1440,128]{2,1,0:T(8,128)(2,1)}, u32[]{:S(2)}) copy-start(bf16[3,1440,128]{2,1,0:T(8,128)(2,1)} %param.6) | copy-start | bytes 3317764
  (9 other events, 13.6 us)
Sparse Core Ops, SparseCore 0:
  355.2 91.9 all-reduce.5
where the time goes:
time: 472 us; the launch traced here: 464 us
  local copies, waits for them, and re-layouts  142 us (30%)
  waiting for transfers between devices  105 us (22%)
  other arithmetic  87.9 us (19%)
  matrix products  57.6 us (12%)
  loops' own time  29.5 us (6%)
  starting transfers between devices  27 us (6%)
  between operations  15 us (3%)
    psum x1, waiting for transfers between devices, body(): lax.psum((weight_total * (1.0 / MODES), filter_total * 0.125), 'space')  92.1 us
    while x496, other arithmetic  46.5 us
    another operation x1, loops' own time, legendre_rows(): final_carry, stacked = lax.scan(degree_block, start_carry, block_ids)  29.5 us
    convert_element_type x8, local copies, waits for them, and re-layouts, body(): spectrum.astype(jnp.float32) * filter_gain[first_degree:][None, :, None, :]  24.9 us
    unnamed x83, local copies, waits for them, and re-layouts  24.7 us
    mul x3, local copies, waits for them, and re-layouts, fourier_tables(): synthesis = analysis * jnp.repeat(doubling, 2)[:, None]  16.5 us
    convert_element_type x2, local copies, waits for them, and re-layouts, fourier_tables(): analysis.reshape(2 * m_order.shape[0], lon_count).astype(jnp.bfloat16)  16.4 us
    dynamic_update_slice x16, local copies, waits for them, and re-layouts, legendre_rows(): final_carry, stacked = lax.scan(degree_block, start_carry, block_ids)  13.6 us
  transfers between devices with their start and end apart: 5, of which 3 were waited for; matrix products, arithmetic and copies ran while one was open for 33% of the time, Pallas kernels for 0%

commit v1 on v0

v1 whole, which is shorter than its diff:
```python
import functools
import math

import jax
import jax.numpy as jnp
import ml_dtypes
import numpy as np
from jax import lax
from jax.experimental import pallas as pl
from jax.experimental.pallas import tpu as pltpu
from jax.sharding import PartitionSpec as P

MODES = 512
TABLE_BYTES = 64 * 1024 * 1024
VMEM_BYTES = 18 * 1024 * 1024
DELAY = 2
BF16 = jnp.bfloat16
F32 = jnp.float32


def latitude_angles(lat_count):
    lat_index = jnp.arange(lat_count, dtype=jnp.float32)
    return math.pi * (lat_index + 0.5) / lat_count


def legendre_rows(m_values, lat_count, mode_count):
    angles = latitude_angles(lat_count)
    cosine = jnp.cos(angles)[None, :]
    sine_lat = jnp.sin(angles)[None, :]
    orders = m_values.astype(jnp.float32)[:, None]
    log_start = 0.5 * (jnp.log(2.0 * orders + 1.0) - math.log(2.0))
    log_start = log_start + 0.5 * (
        lax.lgamma(2.0 * orders + 1.0) - 2.0 * lax.lgamma(orders + 1.0) - orders * math.log(4.0)
    )
    log_start = log_start + orders * jnp.log(sine_lat)

    def degree_block(carry, block_index):
        p_now, p_prev, log_scale = carry
        outputs = []
        for inner_step in range(32):
            degree = (block_index * 32 + inner_step).astype(jnp.float32)
            active = degree > orders
            denom = jnp.maximum(degree * degree - orders * orders, 1.0)
            coef_a = jnp.sqrt((4.0 * degree * degree - 1.0) / denom)
            lower = jnp.maximum((degree - 1.0) * (degree - 1.0) - orders * orders, 0.0)
            coef_b = jnp.sqrt(
                lower * (2.0 * degree + 1.0) / (jnp.maximum(2.0 * degree - 3.0, 1.0) * denom)
            )
            p_next = jnp.where(active, coef_a * cosine * p_now - coef_b * p_prev, p_now)
            p_prev = jnp.where(active, p_now, p_prev)
            p_now = p_next
            outputs.append(jnp.where(degree >= orders, p_now * jnp.exp(log_scale), 0.0))
        magnitude = jnp.maximum(jnp.abs(p_now), jnp.abs(p_prev))
        next_carry = (p_now / magnitude, p_prev / magnitude, log_scale + jnp.log(magnitude))
        return (next_carry, jnp.stack(outputs, 1))

    ones_grid = jnp.ones((m_values.shape[0], lat_count), jnp.float32)
    start_carry = (ones_grid, jnp.zeros_like(ones_grid), log_start * ones_grid)
    block_ids = jnp.arange(mode_count // 32, dtype=jnp.int32)
    final_carry, stacked = lax.scan(degree_block, start_carry, block_ids)
    return jnp.transpose(stacked, (1, 0, 2, 3)).reshape(m_values.shape[0], mode_count, lat_count)


@functools.lru_cache(maxsize=2)
def legendre_constant(lat_count, mode_count):
    angles = np.pi * (np.arange(lat_count) + 0.5) / lat_count
    cosine = np.cos(angles)[None, :]
    orders = np.arange(mode_count, dtype=np.float64)[:, None]
    gamma_2m = np.array([math.lgamma(2.0 * m + 1.0) for m in range(mode_count)])[:, None]
    gamma_m = np.array([math.lgamma(m + 1.0) for m in range(mode_count)])[:, None]
    log_scale = 0.5 * np.log((2.0 * orders + 1.0) / 2.0)
    log_scale = log_scale + 0.5 * (gamma_2m - 2.0 * gamma_m - orders * math.log(4.0))
    log_scale = log_scale + orders * np.log(np.sin(angles))[None, :]
    p_now, p_prev = np.ones_like(log_scale), np.zeros_like(log_scale)
    table = np.zeros((mode_count, mode_count, lat_count), ml_dtypes.bfloat16)
    for degree in range(mode_count):
        active = degree > orders
        denom = np.maximum(degree * degree - orders * orders, 1.0)
        coef_a = np.sqrt(max(4.0 * degree * degree - 1.0, 0.0) / denom)
        lower = np.maximum((degree - 1.0) ** 2 - orders * orders, 0.0)
        coef_b = np.sqrt(lower * (2.0 * degree + 1.0) / (max(2.0 * degree - 3.0, 1.0) * denom))
        p_next = np.where(active, coef_a * cosine * p_now - coef_b * p_prev, p_now)
        p_prev = np.where(active, p_now, p_prev)
        p_now = p_next
        value = np.where(degree >= orders, p_now * np.exp(log_scale), 0.0)
        table[:, degree, :] = value.astype(np.float32).astype(ml_dtypes.bfloat16)
        if degree % 32 == 31:
            magnitude = np.maximum(np.abs(p_now), np.abs(p_prev))
            p_now, p_prev = p_now / magnitude, p_prev / magnitude
            log_scale = log_scale + np.log(magnitude)
    return table


@functools.lru_cache(maxsize=2)
def fourier_constant(devices, lon_count):
    half, slots = lon_count // 2, MODES // devices
    tables = []
    for parity in range(2):
        owner = 2 * np.arange(devices // 2)[:, None] + parity
        orders = (np.arange(slots)[None, :] * devices + owner).reshape(-1)
        phases = (orders[None, :] * np.arange(half)[:, None]) % lon_count
        angles = 2.0 * np.pi / lon_count * phases
        both = np.concatenate([np.cos(angles), -np.sin(angles)], 1) / math.sqrt(lon_count)
        tables.append(both.astype(np.float32).astype(ml_dtypes.bfloat16))
    table = np.stack(tables, 0)
    return np.ascontiguousarray(table), np.ascontiguousarray(table.transpose(0, 2, 1))


def degree_starts(devices):
    firsts = [slot * devices // 16 * 16 for slot in range(MODES // devices)]
    rows = [MODES - first for first in firsts]
    offsets = [sum(rows[:slot]) for slot in range(len(rows))]
    return firsts, offsets, sum(rows)


@functools.lru_cache(maxsize=2)
def packed_legendre(devices, lat_count):
    firsts, offsets, total = degree_starts(devices)
    table = legendre_constant(lat_count, MODES)
    packed = np.concatenate(
        [
            table[slot * devices : (slot + 1) * devices, first:]
            for slot, first in enumerate(firsts)
        ],
        1,
    )
    return np.ascontiguousarray(packed), np.ascontiguousarray(packed.transpose(0, 2, 1))


def table_constants(devices, lat_count):
    _, _, total = degree_starts(devices)
    if devices * total * 2 * (lat_count + max(lat_count, 128)) > TABLE_BYTES:
        return None
    return tuple(jnp.asarray(table) for table in packed_legendre(devices, lat_count))


def made_tables(devices, lat_count, me):
    firsts, _, _ = degree_starts(devices)
    slot_orders = jnp.arange(MODES // devices, dtype=jnp.int32) * devices + me
    legendre = legendre_rows(slot_orders, lat_count, MODES).astype(BF16)
    rows = jnp.concatenate([legendre[slot, first:] for slot, first in enumerate(firsts)], 0)
    return rows, rows.T


def mixing_matrix(mix_weight):
    upper = jnp.concatenate([mix_weight[0], mix_weight[1]], 1)
    lower = jnp.concatenate([-mix_weight[1], mix_weight[0]], 1)
    return jnp.concatenate([upper, lower], 0)


def gelu_slope(field):
    return 0.5 * (1.0 + lax.erf(field * (1.0 / math.sqrt(2.0)))) + field * jnp.exp(
        -0.5 * field * field
    ) * (1.0 / math.sqrt(2.0 * math.pi))


def dot(left, right):
    return jnp.dot(left, right, preferred_element_type=F32)


def row_chunks(count):
    size = count // 3 if count % 48 == 0 else count
    return [(start, size) for start in range(0, count, size)]


def store_rows(out_ref, slots, parity, lat, part, value):
    start = (2 * lat + part) * slots
    out_ref[:, parity, start : start + slots, :] = value.reshape(-1, slots, value.shape[1])


def load_rows(ref, slots, parity, lat, part):
    start = (2 * lat + part) * slots
    return ref[:, parity, start : start + slots, :].reshape(-1, ref.shape[3])


def load_pair(ref, slots, parity, lat):
    return jnp.concatenate([load_rows(ref, slots, parity, lat, part) for part in range(2)], 1)


def fetch_kernel(*refs):
    count = (len(refs) - 1) // 2
    sems = refs[-1]
    copies = [
        pltpu.make_async_copy(refs[index], refs[count + index], sems.at[index])
        for index in range(count)
    ]
    for copy in copies:
        copy.start()
    for copy in copies:
        copy.wait()


def fetch_place_kernel(place_ref, source_hbm, out_ref, sems):
    copy = pltpu.make_async_copy(source_hbm.at[place_ref[0]], out_ref, sems.at[0])
    copy.start()
    copy.wait()


def analyse_kernel(
    slots, grid_hbm, columns_hbm, out_ref, grid_ref, columns_ref, folded_ref, sems
):
    lats, lon_count, channels = grid_ref.shape
    half = lon_count // 2
    block = columns_ref.shape[1] // 2
    grid_copies = [
        pltpu.make_async_copy(grid_hbm.at[lat], grid_ref.at[lat], sems.at[lat])
        for lat in range(lats)
    ]
    table_copies = [
        pltpu.make_async_copy(
            columns_hbm.at[parity, part * block : (part + 1) * block, :],
            columns_ref.at[parity, part * block : (part + 1) * block, :],
            sems.at[lats + 2 * parity + part],
        )
        for parity in range(2)
        for part in range(2)
    ]
    for copy in grid_copies + table_copies:
        copy.start()
    for lat in range(lats):
        grid_copies[lat].wait()
        near = grid_ref[lat, :half, :].astype(F32)
        far = grid_ref[lat, half:, :].astype(F32)
        folded_ref[0, :, lat * channels : (lat + 1) * channels] = (near + far).astype(BF16)
        folded_ref[1, :, lat * channels : (lat + 1) * channels] = (near - far).astype(BF16)
    for parity in range(2):
        for part in range(2):
            table_copies[2 * parity + part].wait()
            result = dot(
                columns_ref[parity, part * block : (part + 1) * block, :], folded_ref[parity]
            ).astype(BF16)
            for lat in range(lats):
                lanes = slice(lat * channels, (lat + 1) * channels)
                store_rows(out_ref, slots, parity, lat, part, result[:, lanes])


def slot_rows(ref, part, slot, slots, lats):
    return ref[pl.ds(part * slots + slot, lats, stride=2 * slots), :]


def slot_pair(ref, slot, slots, lats, scale):
    return jnp.concatenate(
        [(slot_rows(ref, part, slot, slots, lats) * scale).astype(BF16) for part in range(2)], 1
    )


def spread(spread_ref, array_hbm, array_ref, sems, later=()):
    blocks = array_ref.shape[0]
    rows = spread_ref.shape[0] // blocks
    copies = [
        pltpu.make_async_copy(array_hbm.at[block], array_ref.at[block], sems.at[block])
        for block in range(blocks)
    ]
    for copy in [*copies, *later]:
        copy.start()
    for block, copy in enumerate(copies):
        copy.wait()
        spread_ref[block * rows : (block + 1) * rows, :] = array_ref[block].astype(F32)


def staggered(count, delay, first_stage, second_stage):
    waiting = []
    for index in range(count):
        waiting.append((index, first_stage(index)))
        if len(waiting) > delay:
            second_stage(*waiting.pop(0))
    for item in waiting:
        second_stage(*item)


def spectrum_kernel(
    devices,
    rows_ref,
    columns_ref,
    gain_ref,
    weight_ref,
    alpha_ref,
    modes_hbm,
    out_ref,
    modes_ref,
    in_s,
    out_s,
    sems,
):
    slots = MODES // devices
    lats = weight_ref.shape[0]
    firsts, offsets, _ = degree_starts(devices)
    spread(in_s, modes_hbm, modes_ref, sems)
    gain = gain_ref[...]
    channels = gain.shape[1]
    lat_weight = weight_ref[...]

    def forward(slot):
        first, offset = firsts[slot], offsets[slot]
        modes = slot_pair(in_s, slot, slots, lats, lat_weight)
        spectrum = dot(rows_ref[offset : offset + MODES - first, :], modes).astype(BF16)
        return spectrum * jnp.concatenate([gain[first:], gain[first:]], 1)

    def back(slot, scaled):
        first, offset = firsts[slot], offsets[slot]
        result = dot(columns_ref[:, offset : offset + MODES - first], scaled)
        result = result * (alpha_ref[...] if slot == 0 else 2.0)
        for part in range(2):
            out_s[pl.ds(part * slots + slot, lats, stride=2 * slots), :] = result[
                :, part * channels : (part + 1) * channels
            ]

    staggered(slots, DELAY, forward, back)
    out_ref[...] = out_s[...].reshape(out_ref.shape).astype(BF16)


def pairs_kernel(devices, weight_ref, modes_hbm, out_ref, modes_ref, in_s, sems):
    slots = MODES // devices
    lats = weight_ref.shape[0]
    spread(in_s, modes_hbm, modes_ref, sems)
    lat_weight = weight_ref[...]
    for slot in range(slots):
        out_ref[slot * lats : (slot + 1) * lats, :] = slot_pair(
            in_s, slot, slots, lats, lat_weight
        )


def gradient_kernel(
    devices,
    pairs_ref,
    rows_ref,
    gain_ref,
    weight_ref,
    alpha_ref,
    part_ref,
    place_ref,
    grads_hbm,
    columns_hbm,
    out_ref,
    filter_ref,
    grads_ref,
    columns_ref,
    grad_s,
    out_s,
    sems,
    columns_sem,
):
    slots = MODES // devices
    lats = weight_ref.shape[0]
    firsts, offsets, _ = degree_starts(devices)
    columns_copy = pltpu.make_async_copy(
        columns_hbm.at[place_ref[0]], columns_ref, columns_sem.at[0]
    )
    spread(grad_s, grads_hbm, grads_ref, sems, [columns_copy])
    gain = gain_ref[...].astype(F32)
    lat_weight = weight_ref[...]
    channels = gain.shape[1]
    filter_ref[...] = jnp.zeros_like(filter_ref)

    def forward(slot):
        first, offset = firsts[slot], offsets[slot]
        scale = alpha_ref[:, :channels] if slot == 0 else 2.0
        modes = pairs_ref[slot * lats : (slot + 1) * lats, :]
        grads = slot_pair(grad_s, slot, slots, lats, scale)
        table = rows_ref[offset : offset + MODES - first, :]
        spectrum = dot(table, modes)
        gscaled = dot(table, grads)
        product = gscaled * spectrum
        filter_ref[first:, :] += product[:, :channels] + product[:, channels:]
        return (gscaled * jnp.concatenate([gain[first:], gain[first:]], 1)).astype(BF16)

    def back(slot, gspectrum):
        first, offset = firsts[slot], offsets[slot]
        if slot == 0:
            columns_copy.wait()
        result = dot(columns_ref[:, offset : offset + MODES - first], gspectrum)
        for part in range(2):
            out_s[pl.ds(part * slots + slot, lats, stride=2 * slots), :] = (
                result[:, part * channels : (part + 1) * channels] * lat_weight
            )

    staggered(slots, DELAY, forward, back)
    rows = lats // devices * 2 * slots
    out_ref[:, :rows, :] = out_s[...].reshape(devices, rows, channels).astype(BF16)
    if out_ref.shape[1] > rows:
        split = rows + MODES // devices
        out_ref[:, rows:split, :] = (
            filter_ref[...].reshape(devices, MODES // devices, channels).astype(BF16)
        )
        out_ref[:, split:, :] = part_ref[...].reshape(devices, -1, channels).astype(BF16)


def slope_kernel(
    slots,
    modes_ref,
    wide_ref,
    wide_t_ref,
    upstream_ref,
    rows_ref,
    columns_hbm,
    out_ref,
    raw_ref,
    columns_ref,
    modes_s,
    folded_s,
    sems,
):
    columns_copies = [
        pltpu.make_async_copy(columns_hbm.at[parity], columns_ref.at[parity], sems.at[parity])
        for parity in range(2)
    ]
    for copy in columns_copies:
        copy.start()
    lats, lon_count, channels = upstream_ref.shape
    half = lon_count // 2
    block = modes_s.shape[1] // 2
    for parity in range(2):
        for lat in range(lats):
            mixed = dot(load_pair(modes_ref, slots, parity, lat), wide_ref[...]).astype(BF16)
            for part in range(2):
                modes_s[
                    parity,
                    part * block : (part + 1) * block,
                    lat * channels : (lat + 1) * channels,
                ] = mixed[:, part * channels : (part + 1) * channels]
    for start, size in row_chunks(half):
        even = dot(rows_ref[0, start : start + size, :], modes_s[0])
        odd = dot(rows_ref[1, start : start + size, :], modes_s[1])
        for lat in range(lats):
            lanes = slice(lat * channels, (lat + 1) * channels)
            near = upstream_ref[lat, start : start + size, :].astype(F32) * gelu_slope(
                even[:, lanes] + odd[:, lanes]
            )
            far = upstream_ref[lat, half + start : half + start + size, :].astype(
                F32
            ) * gelu_slope(even[:, lanes] - odd[:, lanes])
            folded_s[0, start : start + size, lanes] = (near + far).astype(BF16)
            folded_s[1, start : start + size, lanes] = (near - far).astype(BF16)
    for parity in range(2):
        columns_copies[parity].wait()
        parts = [
            dot(
                columns_ref[parity, part * block : (part + 1) * block, :], folded_s[parity]
            ).astype(BF16)
            for part in range(2)
        ]
        for lat in range(lats):
            lanes = slice(lat * channels, (lat + 1) * channels)
            pair = jnp.concatenate([parts[0][:, lanes], parts[1][:, lanes]], 1)
            mixed = dot(pair, wide_t_ref[...]).astype(BF16)
            for part in range(2):
                store_rows(raw_ref, slots, parity, lat, part, parts[part][:, lanes])
                store_rows(
                    out_ref,
                    slots,
                    parity,
                    lat,
                    part,
                    mixed[:, part * channels : (part + 1) * channels],
                )


def weight_kernel(slots, modes_ref, grad_ref, out_ref):
    channels = modes_ref.shape[3]
    total = jnp.zeros((2 * channels, 2 * channels), F32)
    for parity in range(2):
        for lat in range(modes_ref.shape[2] // (2 * slots)):
            total = total + lax.dot_general(
                load_pair(modes_ref, slots, parity, lat),
                load_pair(grad_ref, slots, parity, lat),
                (((0,), (0,)), ((), ())),
                preferred_element_type=F32,
            )
    out_ref[:channels, :] = total[:channels, :channels] + total[channels:, channels:]
    out_ref[channels:, :] = total[:channels, channels:] - total[channels:, :channels]


def synthesis_kernel(
    slots, modes_ref, upstream_hbm, rows_hbm, out_ref, upstream_ref, rows_ref, modes_s, sems
):
    lats, lon_count, channels = upstream_ref.shape
    copies = [
        pltpu.make_async_copy(rows_hbm.at[parity], rows_ref.at[parity], sems.at[parity])
        for parity in range(2)
    ]
    copies += [
        pltpu.make_async_copy(upstream_hbm.at[lat], upstream_ref.at[lat], sems.at[2 + lat])
        for lat in range(lats)
    ]
    for copy in copies:
        copy.start()
    half = lon_count // 2
    block = modes_s.shape[1] // 2
    for parity in range(2):
        for part in range(2):
            for lat in range(lats):
                modes_s[
                    parity,
                    part * block : (part + 1) * block,
                    lat * channels : (lat + 1) * channels,
                ] = load_rows(modes_ref, slots, parity, lat, part)
    for copy in copies:
        copy.wait()
    for start, size in row_chunks(half):
        even = dot(rows_ref[0, start : start + size, :], modes_s[0])
        odd = dot(rows_ref[1, start : start + size, :], modes_s[1])
        for lat in range(lats):
            lanes = slice(lat * channels, (lat + 1) * channels)
            for sign, base in ((1.0, start), (-1.0, half + start)):
                total = even[:, lanes] + sign * odd[:, lanes]
                total = total + upstream_ref[lat, base : base + size, :].astype(F32)
                out_ref[lat, base : base + size, :] = total.astype(BF16)


def total_kernel(received_ref, out_ref):
    rows = out_ref.shape[1]
    start = received_ref.shape[1] - rows
    total = received_ref[0, start:, :].astype(F32)
    for device in range(1, received_ref.shape[0]):
        total = total + received_ref[device, start:, :].astype(F32)
    out_ref[...] = jnp.broadcast_to(total.astype(BF16)[None], out_ref.shape)


def call(kernel, out_shape, scratch, flops, operands, streamed=()):
    outs = out_shape if isinstance(out_shape, (list, tuple)) else [out_shape]
    moved = sum(2 * math.prod(array.shape) for array in [*operands, *streamed, *outs])
    vmem = pl.BlockSpec(memory_space=pltpu.VMEM)
    return pl.pallas_call(
        kernel,
        out_shape=out_shape,
        in_specs=[
            pl.BlockSpec(memory_space=pltpu.SMEM if array.dtype == jnp.int32 else pltpu.VMEM)
            for array in operands
        ]
        + [pl.BlockSpec(memory_space=pl.ANY)] * len(streamed),
        out_specs=jax.tree.map(lambda _: vmem, out_shape),
        scratch_shapes=scratch,
        cost_estimate=pl.CostEstimate(flops=flops, bytes_accessed=moved, transcendentals=0),
        compiler_params=pltpu.CompilerParams(vmem_limit_bytes=VMEM_BYTES),
    )(*operands, *(away(array) for array in streamed))


def away(array):
    return pltpu.with_memory_space_constraint(array, pltpu.HBM)


def held(array):
    return pltpu.with_memory_space_constraint(array, pltpu.VMEM)


def exchange(array):
    return lax.all_to_all(array, "space", split_axis=0, concat_axis=0, tiled=True)


def sum_over_space(array, devices):
    step = devices // 2
    while step:
        array = array + lax.ppermute(
            array, "space", [(index, index ^ step) for index in range(devices)]
        )
        step //= 2
    return array


def body(grid_in, upstream, mix_weight, degree_filter):
    devices = lax.axis_size("space")
    me = lax.axis_index("space")
    lats, lon_count, channels = grid_in.shape
    lat_count = lats * devices
    slots = MODES // devices
    half = lon_count // 2
    dft_rows, dft_columns = (jnp.asarray(t) for t in fourier_constant(devices, lon_count))
    constants = table_constants(devices, lat_count)
    if constants is None:
        leg_tables = made = made_tables(devices, lat_count, me)
    else:
        leg_tables = [lax.dynamic_index_in_dim(t, me, 0, keepdims=False) for t in constants]
    angles = np.pi * (np.arange(lat_count) + 0.5) / lat_count
    lat_weight = jnp.asarray(
        np.broadcast_to((np.pi / lat_count * np.sin(angles))[:, None], (lat_count, channels)), F32
    )
    alpha = jnp.where(me == 0, 1.0, 2.0) * jnp.ones((1, 2 * channels), F32)
    wide = mixing_matrix(mix_weight)
    mode_rows = lats * 2 * slots
    grid_shape = jax.ShapeDtypeStruct((devices // 2, 2, mode_rows, channels), BF16)
    grid_out = pltpu.HBM(grid_shape.shape, BF16)
    block_shape = (devices, mode_rows, channels)
    mode_shape = jax.ShapeDtypeStruct((lat_count, 2 * slots, channels), BF16)
    spread_shape = pltpu.VMEM((lat_count * 2 * slots, channels), F32)
    modes_scratch = pltpu.VMEM((2, MODES, lats * channels), BF16)
    folded_scratch = pltpu.VMEM((2, half, lats * channels), BF16)
    dft_flops = 2 * MODES * lon_count * lats * channels
    leg_flops = 4 * degree_starts(devices)[2] * lat_count * channels
    modes_shape = (devices, mode_rows, channels)
    modes_landing = pltpu.VMEM(modes_shape, BF16)
    block_sems = pltpu.SemaphoreType.DMA((devices,))
    weight_rows = 2 * channels // devices
    extra = MODES // devices + weight_rows
    joined = (MODES // devices) % 16 == 0 and weight_rows % 16 == 0

    fourier = call(
        functools.partial(analyse_kernel, slots),
        grid_out,
        [
            pltpu.VMEM(grid_in.shape, BF16),
            pltpu.VMEM(dft_columns.shape, BF16),
            folded_scratch,
            pltpu.SemaphoreType.DMA((lats + 4,)),
        ],
        dft_flops,
        [],
        [grid_in, dft_columns],
    )
    held_upstream, held_rows = (
        held(
            call(
                fetch_kernel,
                pltpu.VMEM(array.shape, array.dtype),
                [pltpu.SemaphoreType.DMA((1,))],
                0,
                [],
                [array],
            )
        )
        for array in (upstream, dft_rows)
    )
    modes = exchange(fourier.reshape(block_shape))
    returned = call(
        functools.partial(spectrum_kernel, devices),
        pltpu.HBM(mode_shape.shape, BF16),
        [modes_landing, spread_shape, spread_shape, block_sems],
        2 * leg_flops,
        [*(held(table) for table in leg_tables), degree_filter, lat_weight, alpha],
        [modes],
    )
    returned = exchange(returned.reshape(block_shape)).reshape(grid_shape.shape)
    mixed_grad, raw_grad = call(
        functools.partial(slope_kernel, slots),
        [grid_out, grid_out],
        [
            pltpu.VMEM(dft_columns.shape, BF16),
            modes_scratch,
            folded_scratch,
            pltpu.SemaphoreType.DMA((2,)),
        ],
        2 * dft_flops,
        [away(returned), wide, wide.T, held_upstream, held_rows],
        [dft_columns],
    )
    late_place, mixed_grad = lax.optimization_barrier((me.reshape(1), mixed_grad))
    if constants is None:
        late_rows, late_columns = made[0], made[1][None]
        late_place = jnp.zeros_like(late_place)
    else:
        late_columns = constants[1]
        late_rows = call(
            fetch_place_kernel,
            pltpu.VMEM(constants[0].shape[1:], BF16),
            [pltpu.SemaphoreType.DMA((1,))],
            0,
            [late_place],
            [constants[0]],
        )
    late_modes, mixed_grad = lax.optimization_barrier((modes, mixed_grad))
    pairs = call(
        functools.partial(pairs_kernel, devices),
        pltpu.VMEM((lat_count * slots, 2 * channels), BF16),
        [modes_landing, spread_shape, block_sems],
        0,
        [lat_weight],
        [late_modes],
    )
    grads = exchange(mixed_grad.reshape(block_shape))
    weight_part = call(
        functools.partial(weight_kernel, slots),
        jax.ShapeDtypeStruct((2 * channels, channels), F32),
        [],
        4 * 2 * MODES * lats * channels * channels,
        [away(returned), away(raw_grad)],
    )
    gfield, filter_part = call(
        functools.partial(gradient_kernel, devices),
        [
            jax.ShapeDtypeStruct((devices, mode_rows + (extra if joined else 0), channels), BF16),
            jax.ShapeDtypeStruct((MODES, channels), F32),
        ],
        [
            modes_landing,
            pltpu.VMEM(late_columns.shape[1:], BF16),
            spread_shape,
            spread_shape,
            block_sems,
            pltpu.SemaphoreType.DMA((1,)),
        ],
        3 * leg_flops,
        [
            held(pairs),
            held(late_rows),
            degree_filter,
            lat_weight,
            alpha,
            weight_part,
            late_place,
        ],
        [grads, late_columns],
    )
    gfield = exchange(gfield)
    if joined:
        sums = call(
            total_kernel, jax.ShapeDtypeStruct((devices, extra, channels), BF16), [], 0, [gfield]
        )
        sums = exchange(sums).astype(F32)
        filter_sum = sums[:, : MODES // devices].reshape(MODES, channels)
        weight_sum = sums[:, MODES // devices :].reshape(2 * channels, channels)
    else:
        filter_sum = sum_over_space(filter_part, devices)
        weight_sum = sum_over_space(weight_part, devices)
    grad_in = call(
        functools.partial(synthesis_kernel, slots),
        jax.ShapeDtypeStruct(grid_in.shape, BF16),
        [
            pltpu.VMEM(upstream.shape, BF16),
            pltpu.VMEM(dft_rows.shape, BF16),
            modes_scratch,
            pltpu.SemaphoreType.DMA((2 + lats,)),
        ],
        dft_flops,
        [gfield.reshape(devices // 2, 2, -1, channels)],
        [upstream, dft_rows],
    )
    grad_weight = (weight_sum * (1.0 / MODES)).reshape(2, channels, channels)
    return (grad_in, grad_weight, filter_sum * 0.125)


def solution(mesh):
    return jax.shard_map(
        body,
        mesh=mesh,
        in_specs=(P(("groups", "space"), None, None), P(("groups", "space"), None, None), P(), P()),
        out_specs=(P(("groups", "space"), None, None), P("groups", None, None), P("groups", None)),
        check_vma=False,
    )
```

time: 472 us -> 144 us (0.31); the launches traced: 464 us -> 143 us
  local copies, waits for them, and re-layouts: 142 us -> 3.26 us
  other arithmetic: 87.9 us -> 1.45 us
  matrix products: 57.6 us -> 0 us
  waiting for transfers between devices: 105 us -> 49.6 us
  Pallas kernels: 0 us -> 35.5 us
  loops' own time: 29.5 us -> 0 us
  blocking collectives: 0 us -> 29 us
  between operations: 15 us -> 0.84 us
    psum x1 -> x0, waiting for transfers between devices: 92.1 us -> none  [body(): lax.psum((weight_total * (1.0 / MODES), filter_total * 0.125), 'space')]
    dot_general x31 -> x0, matrix products: 57.6 us -> none  [the longest x4 10.7 us: body(): jnp.dot(scaled_rows, wide_weight, preferred_element_type=jnp.float32)]
    convert_element_type x15 -> x0, local copies, waits for them, and re-layouts: 47.3 us -> none  [the longest x8 24.9 us: body(): spectrum.astype(jnp.float32) * filter_gain[first_degree:][None, :, None, :]]
    while x496 -> x0, other arithmetic: 46.5 us -> none
    all_to_all x4, waiting for transfers between devices: 13 us -> 49.6 us  [exchange(): lax.all_to_all(array, 'space', split_axis=0, concat_axis=0, tiled=True)]
    pallas_call x0 -> x11, Pallas kernels: none -> 35.5 us  [call(): pl.pallas_call(kernel, out_shape=out_shape, in_specs=[pl.BlockSpec(memory...]
    another operation x1 -> x0, loops' own time: 29.5 us -> none  [legendre_rows(): final_carry, stacked = lax.scan(degree_block, start_carry, block_ids)]
    all_to_all x0 -> x1, blocking collectives: none -> 29 us  [exchange(): lax.all_to_all(array, 'space', split_axis=0, concat_axis=0, tiled=True)]
  transfers between devices with their start and end apart: 5 -> 4, of which waited for: 3 -> 4; matrix products, arithmetic and copies ran while one was open for 33% -> 2% of each run, Pallas kernels for 0% -> 9%
where the time goes in v1:
time: 144 us; the launch traced here: 143 us
  waiting for transfers between devices  49.6 us (34%)
  Pallas kernels  35.5 us (25%)
  blocking collectives  29 us (20%)
  starting transfers between devices  23.2 us (16%)
  local copies, waits for them, and re-layouts  3.26 us (2%)
  other arithmetic  1.45 us (1%)
    all_to_all x4, waiting for transfers between devices, exchange(): lax.all_to_all(array, 'space', split_axis=0, concat_axis=0, tiled=True)  49.6 us
    pallas_call x11, Pallas kernels, call(): pl.pallas_call(kernel, out_shape=out_shape, in_specs=[pl.BlockSpec(memory...  35.5 us
    all_to_all x1, blocking collectives, exchange(): lax.all_to_all(array, 'space', split_axis=0, concat_axis=0, tiled=True)  29 us
    all_to_all x4, starting transfers between devices, exchange(): lax.all_to_all(array, 'space', split_axis=0, concat_axis=0, tiled=True)  23.2 us
    squeeze x2, local copies, waits for them, and re-layouts, body(): lax.dynamic_index_in_dim(t, me, 0, keepdims=False)  2.91 us
  transfers between devices with their start and end apart: 4, of which 4 were waited for; matrix products, arithmetic and copies ran while one was open for 2% of the time, Pallas kernels for 9%

profile of v1, /device:TPU:0, one launch (start us, length us, event | category | flops | bytes accessed | tf_op | source)
XLA Modules:
  0.0 142.9 jit_solution(13961644401088873376)
XLA Ops:
  0.6 3.8 %shard_map.112 = bf16[8,2,192,128]{3,2,1,0:T(8,128)(2,1)} custom-call(bf16[3,1440,128]{2,1,0:T(8,128)(2,1)} %grid_hbm.1, bf16[2,512,720]{2,1,0:T(8,128)(2,1)} %constant.34.clone.columns_hbm), custom_call_target="tpu_custom_call" | custom-call | flops 566231040 | bytes 3366912 | tf_op jit(solution)/shard_map/pallas_call | solution.py:523
  4.4 7.4 %all-to-all-start = ((bf16[16,192,128]{2,1,0:T(8,128)(2,1)}), bf16[16,192,128]{2,1,0:T(8,128)(2,1)}, u32[]{:S(2)}, u32[]{:S(2)}) async-start(bf16[16,192,128]{2,1,0:T(8,128)(2,1)} %bitcast.19), calls=%async_computation | async-start | bytes 1572864 | tf_op jit(solution)/shard_map/all_to_all | solution.py:547
  11.9 1.2 dynamic-slice_bitcast_fusion.1.columns_ref
  13.1 0.0 copy-start
  13.1 0.0 copy-start.1
  13.1 1.7 %dynamic-slice_bitcast_fusion.rows_ref = bf16[8448,48]{1,0:T(8,128)(2,1)S(1)} fusion(bf16[16,8448,48]{2,1,0:T(8,128)(2,1)} %constant.35.clone.source_hbm, s32[]{:T(128)S(6)} %select_n.10), kind=kLoop, calls=%fused_computation | loop fusion | bytes 1622020 | tf_op jit(solution)/shard_map/jit(dynamic_index_in_dim)/squeeze | solution.py:572
  14.8 15.8 %all-to-all-done.modes_hbm = bf16[16,192,128]{2,1,0:T(8,128)(2,1)} async-done(((bf16[16,192,128]{2,1,0:T(8,128)(2,1)}), bf16[16,192,128]{2,1,0:T(8,128)(2,1)}, u32[]{:S(2)}, u32[]{:S(2)}) %all-to-all-start) | async-done | bytes 786464 | tf_op jit(solution)/shard_map/all_to_all | solution.py:547
  30.6 0.0 copy-done
  30.6 0.0 copy-done.1
  30.6 6.1 %shard_map.113 = bf16[48,64,128]{2,1,0:T(8,128)(2,1)} custom-call(bf16[8448,48]{1,0:T(8,128)(2,1)S(1)} %dynamic-slice_bitcast_fusion.rows_ref, bf16[48,8448]{1,0:T(8,128)(2,1)S(1)} %dynamic-slice_bitcast_fusion.1.columns_ref, bf16[512,128]{1,0:T(8,128)(2,1)S(1)} %copy-done, f32[48,128]{1,0:T(8,128)S(1)} %copy-done.1, f32[1,256]{1,0:T(1,128)S(1)} %mul.22.alpha_ref, ...), custom_call_target="tpu_custom_call" | custom-call | flops 415236096 | bytes 3338752 | tf_op jit(solution)/shard_map/pallas_call | solution.py:523
  36.8 5.5 %all-to-all-start.1 = ((bf16[16,192,128]{2,1,0:T(8,128)(2,1)}), bf16[16,192,128]{2,1,0:T(8,128)(2,1)}, u32[]{:S(2)}, u32[]{:S(2)}) async-start(bf16[16,192,128]{2,1,0:T(8,128)(2,1)} %bitcast.18), calls=%async_computation.1 | async-start | bytes 1572864 | tf_op jit(solution)/shard_map/all_to_all | solution.py:547
  42.3 0.0 copy-done.2
  42.3 0.1 copy.16
  42.4 0.1 copy.15
  42.6 0.1 copy.14.wide_ref
  42.7 1.4 shard_map.115.rows_ref
  44.1 1.3 shard_map.114.upstream_ref
  45.4 15.7 %all-to-all-done.1 = bf16[16,192,128]{2,1,0:T(8,128)(2,1)} async-done(((bf16[16,192,128]{2,1,0:T(8,128)(2,1)}), bf16[16,192,128]{2,1,0:T(8,128)(2,1)}, u32[]{:S(2)}, u32[]{:S(2)}) %all-to-all-start.1) | async-done | bytes 786464 | tf_op jit(solution)/shard_map/all_to_all | solution.py:547
  61.1 5.7 %shard_map.116 = (bf16[8,2,192,128]{3,2,1,0:T(8,128)(2,1)}, bf16[8,2,192,128]{3,2,1,0:T(8,128)(2,1)}) custom-call(bf16[8,2,192,128]{3,2,1,0:T(8,128)(2,1)} %bitcast.5.modes_ref, bf16[256,256]{1,0:T(8,128)(2,1)S(1)} %copy.14.wide_ref, bf16[256,256]{1,0:T(8,128)(2,1)S(1)} %get-tuple-element.17.wide_t_ref, bf16[3,1440,128]{2,1,0:T(8,128)(2,1)S(1)} %shard_map.114.upstream_ref, ...), custom_call_target="tpu_custom_call" | custom-call | flops 1132462080 | bytes 6676480 | tf_op jit(solution)/shard_map/pallas_call | solution.py:523
  66.8 5.5 %all-to-all-start.2 = ((bf16[16,192,128]{2,1,0:T(8,128)(2,1)}), bf16[16,192,128]{2,1,0:T(8,128)(2,1)}, u32[]{:S(2)}, u32[]{:S(2)}) async-start(bf16[16,192,128]{2,1,0:T(8,128)(2,1)} %bitcast.20), calls=%async_computation.2 | async-start | bytes 1572864 | tf_op jit(solution)/shard_map/all_to_all | solution.py:547
  72.3 2.6 %shard_map.117.pairs_ref = bf16[1536,256]{1,0:T(8,128)(2,1)S(1)} custom-call(f32[48,128]{1,0:T(8,128)S(1)} %copy-done.1, bf16[16,192,128]{2,1,0:T(8,128)(2,1)} %all-to-all-done.modes_hbm), custom_call_target="tpu_custom_call" | custom-call | bytes 1585152 | tf_op jit(solution)/shard_map/pallas_call | solution.py:523
  74.9 1.6 %shard_map.118.rows_ref = bf16[8448,48]{1,0:T(8,128)(2,1)S(1)} custom-call(s32[1]{0:T(128)} %bitcast.1.place_ref, bf16[16,8448,48]{2,1,0:T(8,128)(2,1)} %constant.35.clone.source_hbm), custom_call_target="tpu_custom_call" | custom-call | bytes 13787138 | tf_op jit(solution)/shard_map/pallas_call | solution.py:523
  76.5 1.8 %shard_map.119.part_ref = f32[256,128]{1,0:T(8,128)S(1)} custom-call(bf16[8,2,192,128]{3,2,1,0:T(8,128)(2,1)} %bitcast.5.modes_ref, bf16[8,2,192,128]{3,2,1,0:T(8,128)(2,1)} %get-tuple-element.14.grad_ref), custom_call_target="tpu_custom_call" | custom-call | flops 201326592 | bytes 1638400 | tf_op jit(solution)/shard_map/pallas_call | solution.py:523
  78.3 12.8 %all-to-all-done.2.grads_hbm = bf16[16,192,128]{2,1,0:T(8,128)(2,1)} async-done(((bf16[16,192,128]{2,1,0:T(8,128)(2,1)}), bf16[16,192,128]{2,1,0:T(8,128)(2,1)}, u32[]{:S(2)}, u32[]{:S(2)}) %all-to-all-start.2) | async-done | bytes 786464 | tf_op jit(solution)/shard_map/all_to_all | solution.py:547
  91.1 7.0 %shard_map.120 = (bf16[16,240,128]{2,1,0:T(8,128)(2,1)S(1)}, f32[512,128]{1,0:T(8,128)}) custom-call(bf16[1536,256]{1,0:T(8,128)(2,1)S(1)} %shard_map.117.pairs_ref, bf16[8448,48]{1,0:T(8,128)(2,1)S(1)} %shard_map.118.rows_ref, bf16[512,128]{1,0:T(8,128)(2,1)S(1)} %copy-done, f32[48,128]{1,0:T(8,128)S(1)} %copy-done.1, f32[1,256]{1,0:T(1,128)S(1)} %mul.22.alpha_ref, ...), custom_call_target="tpu_custom_call" | custom-call | flops 622854144 | bytes 16683522 | tf_op jit(solution)/shard_map/pallas_call | solution.py:523
  98.1 29.0 %all_to_all.25.received_ref = bf16[16,240,128]{2,1,0:T(8,128)(2,1)S(1)} all-to-all(bf16[16,240,128]{2,1,0:T(8,128)(2,1)S(1)} %get-tuple-element.16), channel_id=1, replica_groups=mesh['groups'=2,'space'=16] {'space'}, dimensions={0} | all-to-all | bytes 1966080 | tf_op jit(solution)/shard_map/all_to_all | solution.py:547
  127.0 0.7 shard_map.122
  127.8 4.7 %all-to-all-start.4 = ((bf16[16,48,128]{2,1,0:T(8,128)(2,1)}), bf16[16,48,128]{2,1,0:T(8,128)(2,1)S(1)}, u32[]{:S(2)}, u32[]{:S(2)}) async-start(bf16[16,48,128]{2,1,0:T(8,128)(2,1)} %shard_map.122), calls=%async_computation.4 | async-start | bytes 393216 | tf_op jit(solution)/shard_map/all_to_all | solution.py:547
  132.5 3.7 %shard_map.121 = bf16[3,1440,128]{2,1,0:T(8,128)(2,1)} custom-call(bf16[8,2,240,128]{3,2,1,0:T(8,128)(2,1)S(1)} %bitcast.17, bf16[3,1440,128]{2,1,0:T(8,128)(2,1)} %upstream_hbm.1, bf16[2,720,512]{2,1,0:T(8,128)(2,1)} %constant.33.clone.refs_0_.rows_hbm), custom_call_target="tpu_custom_call" | custom-call | flops 566231040 | bytes 4669440 | tf_op jit(solution)/shard_map/pallas_call | solution.py:523
  136.2 5.3 %all-to-all-done.4 = bf16[16,48,128]{2,1,0:T(8,128)(2,1)S(1)} async-done(((bf16[16,48,128]{2,1,0:T(8,128)(2,1)}), bf16[16,48,128]{2,1,0:T(8,128)(2,1)S(1)}, u32[]{:S(2)}, u32[]{:S(2)}) %all-to-all-start.4) | async-done | bytes 196640 | tf_op jit(solution)/shard_map/all_to_all | solution.py:547
  141.5 0.7 slice_multiply_fusion
  142.2 0.7 slice_multiply_fusion.1
  (6 shorter events, 0.1 us)
Async XLA Ops:
  4.4 26.2 %all-to-all-start = ((bf16[16,192,128]{2,1,0:T(8,128)(2,1)}), bf16[16,192,128]{2,1,0:T(8,128)(2,1)}, u32[]{:S(2)}, u32[]{:S(2)}) async-start(bf16[16,192,128]{2,1,0:T(8,128)(2,1)} %bitcast.19), calls=%async_computation | async-start | bytes 1572864 | tf_op jit(solution)/shard_map/all_to_all | solution.py:547
  13.1 17.6 %copy-start = (bf16[512,128]{1,0:T(8,128)(2,1)S(1)}, bf16[512,128]{1,0:T(8,128)(2,1)}, u32[]{:S(2)}) copy-start(bf16[512,128]{1,0:T(8,128)(2,1)} %gain_ref.3) | copy-start | bytes 393220
  13.1 17.5 %copy-start.1 = (f32[48,128]{1,0:T(8,128)S(1)}, f32[48,128]{1,0:T(8,128)}, u32[]{:S(2)}) copy-start(f32[48,128]{1,0:T(8,128)} %constant.37.clone.weight_ref) | copy-start | bytes 73732
  30.6 11.7 %copy-start.2 = (bf16[2,128,128]{2,1,0:T(8,128)(2,1)S(1)}, bf16[2,128,128]{2,1,0:T(8,128)(2,1)}, u32[]{:S(2)}) copy-start(bf16[2,128,128]{2,1,0:T(8,128)(2,1)} %param.11) | copy-start | bytes 196612
  36.8 24.3 %all-to-all-start.1 = ((bf16[16,192,128]{2,1,0:T(8,128)(2,1)}), bf16[16,192,128]{2,1,0:T(8,128)(2,1)}, u32[]{:S(2)}, u32[]{:S(2)}) async-start(bf16[16,192,128]{2,1,0:T(8,128)(2,1)} %bitcast.18), calls=%async_computation.1 | async-start | bytes 1572864 | tf_op jit(solution)/shard_map/all_to_all | solution.py:547
  66.8 24.3 %all-to-all-start.2 = ((bf16[16,192,128]{2,1,0:T(8,128)(2,1)}), bf16[16,192,128]{2,1,0:T(8,128)(2,1)}, u32[]{:S(2)}, u32[]{:S(2)}) async-start(bf16[16,192,128]{2,1,0:T(8,128)(2,1)} %bitcast.20), calls=%async_computation.2 | async-start | bytes 1572864 | tf_op jit(solution)/shard_map/all_to_all | solution.py:547
  127.8 13.7 %all-to-all-start.4 = ((bf16[16,48,128]{2,1,0:T(8,128)(2,1)}), bf16[16,48,128]{2,1,0:T(8,128)(2,1)S(1)}, u32[]{:S(2)}, u32[]{:S(2)}) async-start(bf16[16,48,128]{2,1,0:T(8,128)(2,1)} %shard_map.122), calls=%async_computation.4 | async-start | bytes 393216 | tf_op jit(solution)/shard_map/all_to_all | solution.py:547

commit v2 on v1

--- a/solution.py
+++ b/solution.py
@@ -13,7 +13,7 @@
 MODES = 512
 TABLE_BYTES = 64 * 1024 * 1024
 VMEM_BYTES = 18 * 1024 * 1024
-DELAY = 2
+DELAY = 4
 BF16 = jnp.bfloat16
 F32 = jnp.float32
 
@@ -235,7 +235,7 @@
 
 
 def slot_rows(ref, part, slot, slots, lats):
-    return ref[pl.ds(part * slots + slot, lats, stride=2 * slots), :]
+    return ref[pl.ds(part * slots + slot, lats, stride=ref.shape[0] // lats), :]
 
 
 def slot_pair(ref, slot, slots, lats, scale):
@@ -244,18 +244,43 @@
     )
 
 
-def spread(spread_ref, array_hbm, array_ref, sems, later=()):
-    blocks = array_ref.shape[0]
-    rows = spread_ref.shape[0] // blocks
-    copies = [
-        pltpu.make_async_copy(array_hbm.at[block], array_ref.at[block], sems.at[block])
-        for block in range(blocks)
-    ]
-    for copy in [*copies, *later]:
-        copy.start()
-    for block, copy in enumerate(copies):
-        copy.wait()
-        spread_ref[block * rows : (block + 1) * rows, :] = array_ref[block].astype(F32)
+def slot_halves(slots):
+    size = slots // 2 if slots % 32 == 0 else slots
+    return [(start, size) for start in range(0, slots, size)]
+
+
+class Landing:
+    def __init__(self, slots, spread_ref, array_hbm, array_ref, sems):
+        lats, rows, channels = array_ref.shape
+        self.halves = slot_halves(slots)
+        self.spread_ref = spread_ref.reshape(lats, spread_ref.shape[0] // lats, channels)
+        self.array_ref = array_ref
+        self.copies = {}
+        for half, (start, size) in enumerate(self.halves):
+            group = []
+            for part in range(2):
+                span = slice(part * slots + start, part * slots + start + size)
+                if len(self.halves) == 1:
+                    span = slice(0, rows)
+                for piece in range(2):
+                    block = slice(piece * lats // 2, (piece + 1) * lats // 2)
+                    copy = pltpu.make_async_copy(
+                        array_hbm.at[block, span, :],
+                        array_ref.at[block, span, :],
+                        sems.at[4 * half + 2 * part + piece],
+                    )
+                    group.append((copy, block, span))
+                if len(self.halves) == 1:
+                    break
+            self.copies[start] = group
+        for group in self.copies.values():
+            for copy, _, _ in group:
+                copy.start()
+
+    def need(self, slot):
+        for copy, block, span in self.copies.pop(slot, ()):
+            copy.wait()
+            self.spread_ref[block, span, :] = self.array_ref[block, span, :].astype(F32)
 
 
 def staggered(count, delay, first_stage, second_stage):
@@ -276,22 +301,26 @@
     weight_ref,
     alpha_ref,
     modes_hbm,
-    out_ref,
+    out_hbm,
     modes_ref,
     in_s,
     out_s,
+    out_ref,
     sems,
+    out_sems,
 ):
     slots = MODES // devices
     lats = weight_ref.shape[0]
     firsts, offsets, _ = degree_starts(devices)
-    spread(in_s, modes_hbm, modes_ref, sems)
+    landing = Landing(slots, in_s, modes_hbm, modes_ref, sems)
+    stores = []
     gain = gain_ref[...]
     channels = gain.shape[1]
     lat_weight = weight_ref[...]
 
     def forward(slot):
         first, offset = firsts[slot], offsets[slot]
+        landing.need(slot)
         modes = slot_pair(in_s, slot, slots, lats, lat_weight)
         spectrum = dot(rows_ref[offset : offset + MODES - first, :], modes).astype(BF16)
         return spectrum * jnp.concatenate([gain[first:], gain[first:]], 1)
@@ -301,20 +330,41 @@
         result = dot(columns_ref[:, offset : offset + MODES - first], scaled)
         result = result * (alpha_ref[...] if slot == 0 else 2.0)
         for part in range(2):
-            out_s[pl.ds(part * slots + slot, lats, stride=2 * slots), :] = result[
+            out_s[pl.ds(part * slots + slot, lats, stride=out_s.shape[0] // lats), :] = result[
                 :, part * channels : (part + 1) * channels
             ]
+        for start, size in landing.halves:
+            if slot == start + size - 1:
+                store(start, size)
+
+    def store(start, size):
+        view = out_s.reshape(lats, out_s.shape[0] // lats, channels)
+        for part in range(2):
+            span = slice(part * slots + start, part * slots + start + size)
+            out_ref[:, span, :] = view[:, span, :].astype(BF16)
+            if size < slots:
+                copy = pltpu.make_async_copy(
+                    out_ref.at[:, span, :], out_hbm.at[:, span, :], out_sems.at[len(stores)]
+                )
+                copy.start()
+                stores.append(copy)
+        if size == slots:
+            copy = pltpu.make_async_copy(out_ref, out_hbm, out_sems.at[0])
+            copy.start()
+            stores.append(copy)
 
     staggered(slots, DELAY, forward, back)
-    out_ref[...] = out_s[...].reshape(out_ref.shape).astype(BF16)
+    for copy in stores:
+        copy.wait()
 
 
 def pairs_kernel(devices, weight_ref, modes_hbm, out_ref, modes_ref, in_s, sems):
     slots = MODES // devices
     lats = weight_ref.shape[0]
-    spread(in_s, modes_hbm, modes_ref, sems)
+    landing = Landing(slots, in_s, modes_hbm, modes_ref, sems)
     lat_weight = weight_ref[...]
     for slot in range(slots):
+        landing.need(slot)
         out_ref[slot * lats : (slot + 1) * lats, :] = slot_pair(
             in_s, slot, slots, lats, lat_weight
         )
@@ -346,7 +396,8 @@
     columns_copy = pltpu.make_async_copy(
         columns_hbm.at[place_ref[0]], columns_ref, columns_sem.at[0]
     )
-    spread(grad_s, grads_hbm, grads_ref, sems, [columns_copy])
+    landing = Landing(slots, grad_s, grads_hbm, grads_ref, sems)
+    columns_copy.start()
     gain = gain_ref[...].astype(F32)
     lat_weight = weight_ref[...]
     channels = gain.shape[1]
@@ -354,6 +405,7 @@
 
     def forward(slot):
         first, offset = firsts[slot], offsets[slot]
+        landing.need(slot)
         scale = alpha_ref[:, :channels] if slot == 0 else 2.0
         modes = pairs_ref[slot * lats : (slot + 1) * lats, :]
         grads = slot_pair(grad_s, slot, slots, lats, scale)
@@ -370,13 +422,16 @@
             columns_copy.wait()
         result = dot(columns_ref[:, offset : offset + MODES - first], gspectrum)
         for part in range(2):
-            out_s[pl.ds(part * slots + slot, lats, stride=2 * slots), :] = (
+            out_s[pl.ds(part * slots + slot, lats, stride=out_s.shape[0] // lats), :] = (
                 result[:, part * channels : (part + 1) * channels] * lat_weight
             )
 
     staggered(slots, DELAY, forward, back)
     rows = lats // devices * 2 * slots
-    out_ref[:, :rows, :] = out_s[...].reshape(devices, rows, channels).astype(BF16)
+    view = out_s.reshape(lats, out_s.shape[0] // lats, channels)
+    out_ref[:, :rows, :] = (
+        view[:, : 2 * slots, :].astype(BF16).reshape(devices, rows, channels)
+    )
     if out_ref.shape[1] > rows:
         split = rows + MODES // devices
         out_ref[:, rows:split, :] = (
@@ -387,37 +442,54 @@
 
 def slope_kernel(
     slots,
-    modes_ref,
     wide_ref,
     wide_t_ref,
     upstream_ref,
     rows_ref,
+    modes_hbm,
     columns_hbm,
-    out_ref,
-    raw_ref,
+    out_hbm,
+    weight_ref,
+    modes_ref,
     columns_ref,
     modes_s,
     folded_s,
+    out_ref,
     sems,
+    columns_sems,
+    out_sems,
 ):
-    columns_copies = [
-        pltpu.make_async_copy(columns_hbm.at[parity], columns_ref.at[parity], sems.at[parity])
-        for parity in range(2)
-    ]
-    for copy in columns_copies:
-        copy.start()
     lats, lon_count, channels = upstream_ref.shape
     half = lon_count // 2
     block = modes_s.shape[1] // 2
-    for parity in range(2):
-        for lat in range(lats):
-            mixed = dot(load_pair(modes_ref, slots, parity, lat), wide_ref[...]).astype(BF16)
-            for part in range(2):
-                modes_s[
-                    parity,
-                    part * block : (part + 1) * block,
-                    lat * channels : (lat + 1) * channels,
-                ] = mixed[:, part * channels : (part + 1) * channels]
+
+    def lat_copy(source, target, sem_refs, parity, lat):
+        span = slice(2 * lat * slots, 2 * (lat + 1) * slots)
+        return pltpu.make_async_copy(
+            source.at[:, parity, span, :],
+            target.at[:, parity, span, :],
+            sem_refs.at[parity * lats + lat],
+        )
+
+    places = [(parity, lat) for parity in range(2) for lat in range(lats)]
+    modes_copies = [lat_copy(modes_hbm, modes_ref, sems, *place) for place in places]
+    columns_copies = [
+        pltpu.make_async_copy(
+            columns_hbm.at[parity], columns_ref.at[parity], columns_sems.at[parity]
+        )
+        for parity in range(2)
+    ]
+    for copy in modes_copies + columns_copies:
+        copy.start()
+    for (parity, lat), copy in zip(places, modes_copies):
+        copy.wait()
+        mixed = dot(load_pair(modes_ref, slots, parity, lat), wide_ref[...]).astype(BF16)
+        for part in range(2):
+            modes_s[
+                parity,
+                part * block : (part + 1) * block,
+                lat * channels : (lat + 1) * channels,
+            ] = mixed[:, part * channels : (part + 1) * channels]
     for start, size in row_chunks(half):
         even = dot(rows_ref[0, start : start + size, :], modes_s[0])
         odd = dot(rows_ref[1, start : start + size, :], modes_s[1])
@@ -431,6 +503,7 @@
             ) * gelu_slope(even[:, lanes] - odd[:, lanes])
             folded_s[0, start : start + size, lanes] = (near + far).astype(BF16)
             folded_s[1, start : start + size, lanes] = (near - far).astype(BF16)
+    pairs, stores = [], []
     for parity in range(2):
         columns_copies[parity].wait()
         parts = [
@@ -444,7 +517,6 @@
             pair = jnp.concatenate([parts[0][:, lanes], parts[1][:, lanes]], 1)
             mixed = dot(pair, wide_t_ref[...]).astype(BF16)
             for part in range(2):
-                store_rows(raw_ref, slots, parity, lat, part, parts[part][:, lanes])
                 store_rows(
                     out_ref,
                     slots,
@@ -453,21 +525,21 @@
                     part,
                     mixed[:, part * channels : (part + 1) * channels],
                 )
-
-
-def weight_kernel(slots, modes_ref, grad_ref, out_ref):
-    channels = modes_ref.shape[3]
+            stores.append(lat_copy(out_ref, out_hbm, out_sems, parity, lat))
+            stores[-1].start()
+            pairs.append(pair)
     total = jnp.zeros((2 * channels, 2 * channels), F32)
-    for parity in range(2):
-        for lat in range(modes_ref.shape[2] // (2 * slots)):
-            total = total + lax.dot_general(
-                load_pair(modes_ref, slots, parity, lat),
-                load_pair(grad_ref, slots, parity, lat),
-                (((0,), (0,)), ((), ())),
-                preferred_element_type=F32,
-            )
-    out_ref[:channels, :] = total[:channels, :channels] + total[channels:, channels:]
-    out_ref[channels:, :] = total[:channels, channels:] - total[channels:, :channels]
+    for (parity, lat), pair in zip(places, pairs):
+        total = total + lax.dot_general(
+            load_pair(modes_ref, slots, parity, lat),
+            pair,
+            (((0,), (0,)), ((), ())),
+            preferred_element_type=F32,
+        )
+    weight_ref[:channels, :] = total[:channels, :channels] + total[channels:, channels:]
+    weight_ref[channels:, :] = total[:channels, channels:] - total[channels:, :channels]
+    for copy in stores:
+        copy.wait()
 
 
 def synthesis_kernel(
@@ -516,10 +588,24 @@
     out_ref[...] = jnp.broadcast_to(total.astype(BF16)[None], out_ref.shape)
 
 
-def call(kernel, out_shape, scratch, flops, operands, streamed=()):
+def finish_kernel(received_ref, filter_ref, weight_ref):
+    devices, rows, channels = received_ref.shape
+    split = filter_ref.shape[0] // devices
+    filter_ref[...] = (
+        received_ref[:, :split, :].astype(F32).reshape(filter_ref.shape) * 0.125
+    )
+    weight_ref[...] = received_ref[:, split:, :].astype(F32).reshape(weight_ref.shape) * (
+        1.0 / MODES
+    )
+
+
+def call(kernel, out_shape, scratch, flops, operands, streamed=(), written=0):
     outs = out_shape if isinstance(out_shape, (list, tuple)) else [out_shape]
     moved = sum(2 * math.prod(array.shape) for array in [*operands, *streamed, *outs])
-    vmem = pl.BlockSpec(memory_space=pltpu.VMEM)
+    specs = [
+        pl.BlockSpec(memory_space=pl.ANY if index < written else pltpu.VMEM)
+        for index in range(len(outs))
+    ]
     return pl.pallas_call(
         kernel,
         out_shape=out_shape,
@@ -528,7 +614,7 @@
             for array in operands
         ]
         + [pl.BlockSpec(memory_space=pl.ANY)] * len(streamed),
-        out_specs=jax.tree.map(lambda _: vmem, out_shape),
+        out_specs=specs if isinstance(out_shape, (list, tuple)) else specs[0],
         scratch_shapes=scratch,
         cost_estimate=pl.CostEstimate(flops=flops, bytes_accessed=moved, transcendentals=0),
         compiler_params=pltpu.CompilerParams(vmem_limit_bytes=VMEM_BYTES),
@@ -581,14 +667,13 @@
     grid_out = pltpu.HBM(grid_shape.shape, BF16)
     block_shape = (devices, mode_rows, channels)
     mode_shape = jax.ShapeDtypeStruct((lat_count, 2 * slots, channels), BF16)
-    spread_shape = pltpu.VMEM((lat_count * 2 * slots, channels), F32)
+    spread_shape = pltpu.VMEM((lat_count * (2 * slots + 8), channels), F32)
     modes_scratch = pltpu.VMEM((2, MODES, lats * channels), BF16)
     folded_scratch = pltpu.VMEM((2, half, lats * channels), BF16)
     dft_flops = 2 * MODES * lon_count * lats * channels
     leg_flops = 4 * degree_starts(devices)[2] * lat_count * channels
-    modes_shape = (devices, mode_rows, channels)
-    modes_landing = pltpu.VMEM(modes_shape, BF16)
-    block_sems = pltpu.SemaphoreType.DMA((devices,))
+    modes_landing = pltpu.VMEM(mode_shape.shape, BF16)
+    block_sems = pltpu.SemaphoreType.DMA((8,))
     weight_rows = 2 * channels // devices
     extra = MODES // devices + weight_rows
     joined = (MODES // devices) % 16 == 0 and weight_rows % 16 == 0
@@ -619,28 +704,42 @@
         )
         for array in (upstream, dft_rows)
     )
-    modes = exchange(fourier.reshape(block_shape))
+    modes = exchange(fourier.reshape(block_shape)).reshape(mode_shape.shape)
     returned = call(
         functools.partial(spectrum_kernel, devices),
         pltpu.HBM(mode_shape.shape, BF16),
-        [modes_landing, spread_shape, spread_shape, block_sems],
+        [
+            modes_landing,
+            spread_shape,
+            spread_shape,
+            modes_landing,
+            block_sems,
+            pltpu.SemaphoreType.DMA((4,)),
+        ],
         2 * leg_flops,
         [*(held(table) for table in leg_tables), degree_filter, lat_weight, alpha],
         [modes],
+        written=1,
     )
     returned = exchange(returned.reshape(block_shape)).reshape(grid_shape.shape)
-    mixed_grad, raw_grad = call(
+    grid_landing = pltpu.VMEM(grid_shape.shape, BF16)
+    mixed_grad, weight_part = call(
         functools.partial(slope_kernel, slots),
-        [grid_out, grid_out],
+        [grid_out, jax.ShapeDtypeStruct((2 * channels, channels), F32)],
         [
+            grid_landing,
             pltpu.VMEM(dft_columns.shape, BF16),
             modes_scratch,
             folded_scratch,
+            grid_landing,
+            pltpu.SemaphoreType.DMA((2 * lats,)),
             pltpu.SemaphoreType.DMA((2,)),
+            pltpu.SemaphoreType.DMA((2 * lats,)),
         ],
         2 * dft_flops,
-        [away(returned), wide, wide.T, held_upstream, held_rows],
-        [dft_columns],
+        [wide, wide.T, held_upstream, held_rows],
+        [returned, dft_columns],
+        written=1,
     )
     late_place, mixed_grad = lax.optimization_barrier((me.reshape(1), mixed_grad))
     if constants is None:
@@ -665,14 +764,7 @@
         [lat_weight],
         [late_modes],
     )
-    grads = exchange(mixed_grad.reshape(block_shape))
-    weight_part = call(
-        functools.partial(weight_kernel, slots),
-        jax.ShapeDtypeStruct((2 * channels, channels), F32),
-        [],
-        4 * 2 * MODES * lats * channels * channels,
-        [away(returned), away(raw_grad)],
-    )
+    grads = exchange(mixed_grad.reshape(block_shape)).reshape(mode_shape.shape)
     gfield, filter_part = call(
         functools.partial(gradient_kernel, devices),
         [
@@ -704,12 +796,19 @@
         sums = call(
             total_kernel, jax.ShapeDtypeStruct((devices, extra, channels), BF16), [], 0, [gfield]
         )
-        sums = exchange(sums).astype(F32)
-        filter_sum = sums[:, : MODES // devices].reshape(MODES, channels)
-        weight_sum = sums[:, MODES // devices :].reshape(2 * channels, channels)
+        grad_filter, grad_weight = call(
+            finish_kernel,
+            [
+                jax.ShapeDtypeStruct((MODES, channels), F32),
+                jax.ShapeDtypeStruct((2 * channels, channels), F32),
+            ],
+            [],
+            0,
+            [exchange(sums)],
+        )
     else:
-        filter_sum = sum_over_space(filter_part, devices)
-        weight_sum = sum_over_space(weight_part, devices)
+        grad_filter = sum_over_space(filter_part, devices) * 0.125
+        grad_weight = sum_over_space(weight_part, devices) * (1.0 / MODES)
     grad_in = call(
         functools.partial(synthesis_kernel, slots),
         jax.ShapeDtypeStruct(grid_in.shape, BF16),
@@ -723,8 +822,7 @@
         [gfield.reshape(devices // 2, 2, -1, channels)],
         [upstream, dft_rows],
     )
-    grad_weight = (weight_sum * (1.0 / MODES)).reshape(2, channels, channels)
-    return (grad_in, grad_weight, filter_sum * 0.125)
+    return (grad_in, grad_weight.reshape(2, channels, channels), grad_filter)
 
 
 def solution(mesh):

time: 144 us -> 140 us (0.972)
  Pallas kernels: 35.5 us -> 30.4 us
  waiting for transfers between devices: 49.6 us -> 52.5 us
    pallas_call x11, Pallas kernels: 35.5 us -> 30.4 us  [call(): pl.pallas_call(kernel, out_shape=out_shape, in_specs=[pl.BlockSpec(memory...]
    all_to_all x4, waiting for transfers between devices: 49.6 us -> 52.5 us  [exchange(): lax.all_to_all(array, 'space', split_axis=0, concat_axis=0, tiled=True)]
  transfers between devices with their start and end apart: 4 -> 4, of which waited for: 4 -> 4; matrix products, arithmetic and copies ran while one was open for 2% -> 2% of each run, Pallas kernels for 9% -> 7%
where the time goes in v2:
time: 140 us; the launch traced here: 139 us
  waiting for transfers between devices  52.5 us (38%)
  Pallas kernels  30.4 us (22%)
  blocking collectives  29 us (21%)
  starting transfers between devices  23.3 us (17%)
  local copies, waits for them, and re-layouts  3.26 us (2%)
    all_to_all x4, waiting for transfers between devices, exchange(): lax.all_to_all(array, 'space', split_axis=0, concat_axis=0, tiled=True)  52.5 us
    pallas_call x11, Pallas kernels, call(): pl.pallas_call(kernel, out_shape=out_shape, in_specs=[pl.BlockSpec(memory...  30.4 us
    all_to_all x1, blocking collectives, exchange(): lax.all_to_all(array, 'space', split_axis=0, concat_axis=0, tiled=True)  29 us
    all_to_all x4, starting transfers between devices, exchange(): lax.all_to_all(array, 'space', split_axis=0, concat_axis=0, tiled=True)  23.3 us
    squeeze x2, local copies, waits for them, and re-layouts, body(): lax.dynamic_index_in_dim(t, me, 0, keepdims=False)  2.91 us
  transfers between devices with their start and end apart: 4, of which 4 were waited for; matrix products, arithmetic and copies ran while one was open for 2% of the time, Pallas kernels for 7%

profile of v2, /device:TPU:0, one launch (start us, length us, event | category | flops | bytes accessed | tf_op | source)
XLA Modules:
  0.0 139.2 jit_solution(7815929255598117131)
XLA Ops:
  0.6 3.8 %shard_map.112 = bf16[8,2,192,128]{3,2,1,0:T(8,128)(2,1)} custom-call(bf16[3,1440,128]{2,1,0:T(8,128)(2,1)} %grid_hbm.1, bf16[2,512,720]{2,1,0:T(8,128)(2,1)} %constant.30.clone.columns_hbm), custom_call_target="tpu_custom_call" | custom-call | flops 566231040 | bytes 3366912 | tf_op jit(solution)/shard_map/pallas_call | solution.py:609
  4.4 7.4 %all-to-all-start = ((bf16[16,192,128]{2,1,0:T(8,128)(2,1)}), bf16[16,192,128]{2,1,0:T(8,128)(2,1)}, u32[]{:S(2)}, u32[]{:S(2)}) async-start(bf16[16,192,128]{2,1,0:T(8,128)(2,1)} %bitcast.20), calls=%async_computation | async-start | bytes 1572864 | tf_op jit(solution)/shard_map/all_to_all | solution.py:633
  11.9 1.2 dynamic-slice_bitcast_fusion.1.columns_ref
  13.1 0.0 copy-start
  13.1 0.0 copy-start.1
  13.1 1.7 %dynamic-slice_bitcast_fusion.rows_ref = bf16[8448,48]{1,0:T(8,128)(2,1)S(1)} fusion(bf16[16,8448,48]{2,1,0:T(8,128)(2,1)} %constant.31.clone.source_hbm, s32[]{:T(128)S(6)} %select_n.10), kind=kLoop, calls=%fused_computation | loop fusion | bytes 1622020 | tf_op jit(solution)/shard_map/jit(dynamic_index_in_dim)/squeeze | solution.py:658
  14.8 15.8 %all-to-all-done = bf16[16,192,128]{2,1,0:T(8,128)(2,1)} async-done(((bf16[16,192,128]{2,1,0:T(8,128)(2,1)}), bf16[16,192,128]{2,1,0:T(8,128)(2,1)}, u32[]{:S(2)}, u32[]{:S(2)}) %all-to-all-start) | async-done | bytes 786464 | tf_op jit(solution)/shard_map/all_to_all | solution.py:633
  30.6 0.0 copy-done
  30.6 0.0 copy-done.1
  30.6 0.0 copy-start.2
  30.6 4.4 %shard_map.115 = bf16[48,64,128]{2,1,0:T(8,128)(2,1)} custom-call(bf16[8448,48]{1,0:T(8,128)(2,1)S(1)} %dynamic-slice_bitcast_fusion.rows_ref, bf16[48,8448]{1,0:T(8,128)(2,1)S(1)} %dynamic-slice_bitcast_fusion.1.columns_ref, bf16[512,128]{1,0:T(8,128)(2,1)S(1)} %copy-done, f32[48,128]{1,0:T(8,128)S(1)} %copy-done.1, f32[1,256]{1,0:T(1,128)S(1)} %mul.3.alpha_ref, ...), custom_call_target="tpu_custom_call" | custom-call | flops 415236096 | bytes 3338752 | tf_op jit(solution)/shard_map/pallas_call | solution.py:609
  35.0 5.5 %all-to-all-start.1 = ((bf16[16,192,128]{2,1,0:T(8,128)(2,1)}), bf16[16,192,128]{2,1,0:T(8,128)(2,1)}, u32[]{:S(2)}, u32[]{:S(2)}) async-start(bf16[16,192,128]{2,1,0:T(8,128)(2,1)} %bitcast.19), calls=%async_computation.1 | async-start | bytes 1572864 | tf_op jit(solution)/shard_map/all_to_all | solution.py:633
  40.6 0.0 copy-done.2
  40.6 0.1 copy.16
  40.7 0.1 copy.15
  40.9 0.1 copy.14.wide_ref
  41.0 1.4 shard_map.114.rows_ref
  42.4 1.3 shard_map.113.upstream_ref
  43.6 15.7 %all-to-all-done.1 = bf16[16,192,128]{2,1,0:T(8,128)(2,1)} async-done(((bf16[16,192,128]{2,1,0:T(8,128)(2,1)}), bf16[16,192,128]{2,1,0:T(8,128)(2,1)}, u32[]{:S(2)}, u32[]{:S(2)}) %all-to-all-start.1) | async-done | bytes 786464 | tf_op jit(solution)/shard_map/all_to_all | solution.py:633
  59.3 6.1 %shard_map.116 = (bf16[8,2,192,128]{3,2,1,0:T(8,128)(2,1)}, f32[256,128]{1,0:T(8,128)S(1)}) custom-call(bf16[256,256]{1,0:T(8,128)(2,1)S(1)} %copy.14.wide_ref, bf16[256,256]{1,0:T(8,128)(2,1)S(1)} %get-tuple-element.21.wide_t_ref, bf16[3,1440,128]{2,1,0:T(8,128)(2,1)S(1)} %shard_map.113.upstream_ref, bf16[2,720,512]{2,1,0:T(8,128)(2,1)S(1)} %shard_map.114.rows_ref, ...), custom_call_target="tpu_custom_call" | custom-call | flops 1132462080 | bytes 5955584 | tf_op jit(solution)/shard_map/pallas_call | solution.py:609
  65.5 5.5 %all-to-all-start.2 = ((bf16[16,192,128]{2,1,0:T(8,128)(2,1)}), bf16[16,192,128]{2,1,0:T(8,128)(2,1)}, u32[]{:S(2)}, u32[]{:S(2)}) async-start(bf16[16,192,128]{2,1,0:T(8,128)(2,1)} %bitcast.21), calls=%async_computation.2 | async-start | bytes 1572864 | tf_op jit(solution)/shard_map/all_to_all | solution.py:633
  71.0 1.4 %shard_map.117.pairs_ref = bf16[1536,256]{1,0:T(8,128)(2,1)S(1)} custom-call(f32[48,128]{1,0:T(8,128)S(1)} %copy-done.1, bf16[48,64,128]{2,1,0:T(8,128)(2,1)} %bitcast.1.modes_hbm), custom_call_target="tpu_custom_call" | custom-call | bytes 1585152 | tf_op jit(solution)/shard_map/pallas_call | solution.py:609
  72.5 1.6 %shard_map.118.rows_ref = bf16[8448,48]{1,0:T(8,128)(2,1)S(1)} custom-call(s32[1]{0:T(128)} %bitcast.2.place_ref, bf16[16,8448,48]{2,1,0:T(8,128)(2,1)} %constant.31.clone.source_hbm), custom_call_target="tpu_custom_call" | custom-call | bytes 13787138 | tf_op jit(solution)/shard_map/pallas_call | solution.py:609
  74.1 15.7 %all-to-all-done.2 = bf16[16,192,128]{2,1,0:T(8,128)(2,1)} async-done(((bf16[16,192,128]{2,1,0:T(8,128)(2,1)}), bf16[16,192,128]{2,1,0:T(8,128)(2,1)}, u32[]{:S(2)}, u32[]{:S(2)}) %all-to-all-start.2) | async-done | bytes 786464 | tf_op jit(solution)/shard_map/all_to_all | solution.py:633
  89.8 5.2 %shard_map.119 = (bf16[16,240,128]{2,1,0:T(8,128)(2,1)S(1)}, f32[512,128]{1,0:T(8,128)}) custom-call(bf16[1536,256]{1,0:T(8,128)(2,1)S(1)} %shard_map.117.pairs_ref, bf16[8448,48]{1,0:T(8,128)(2,1)S(1)} %shard_map.118.rows_ref, bf16[512,128]{1,0:T(8,128)(2,1)S(1)} %copy-done, f32[48,128]{1,0:T(8,128)S(1)} %copy-done.1, f32[1,256]{1,0:T(1,128)S(1)} %mul.3.alpha_ref, ...), custom_call_target="tpu_custom_call" | custom-call | flops 622854144 | bytes 16683522 | tf_op jit(solution)/shard_map/pallas_call | solution.py:609
  95.0 29.0 %all_to_all.25.received_ref = bf16[16,240,128]{2,1,0:T(8,128)(2,1)S(1)} all-to-all(bf16[16,240,128]{2,1,0:T(8,128)(2,1)S(1)} %get-tuple-element.18), channel_id=1, replica_groups=mesh['groups'=2,'space'=16] {'space'}, dimensions={0} | all-to-all | bytes 1966080 | tf_op jit(solution)/shard_map/all_to_all | solution.py:633
  124.0 0.7 shard_map.121
  124.7 4.7 %all-to-all-start.4 = ((bf16[16,48,128]{2,1,0:T(8,128)(2,1)}), bf16[16,48,128]{2,1,0:T(8,128)(2,1)S(1)}, u32[]{:S(2)}, u32[]{:S(2)}) async-start(bf16[16,48,128]{2,1,0:T(8,128)(2,1)} %shard_map.121), calls=%async_computation.4 | async-start | bytes 393216 | tf_op jit(solution)/shard_map/all_to_all | solution.py:633
  129.4 3.7 %shard_map.120 = bf16[3,1440,128]{2,1,0:T(8,128)(2,1)} custom-call(bf16[8,2,240,128]{3,2,1,0:T(8,128)(2,1)S(1)} %bitcast.18, bf16[3,1440,128]{2,1,0:T(8,128)(2,1)} %upstream_hbm.1, bf16[2,720,512]{2,1,0:T(8,128)(2,1)} %constant.29.clone.refs_0_.rows_hbm), custom_call_target="tpu_custom_call" | custom-call | flops 566231040 | bytes 4669440 | tf_op jit(solution)/shard_map/pallas_call | solution.py:609
  133.1 5.3 %all-to-all-done.4.received_ref = bf16[16,48,128]{2,1,0:T(8,128)(2,1)S(1)} async-done(((bf16[16,48,128]{2,1,0:T(8,128)(2,1)}), bf16[16,48,128]{2,1,0:T(8,128)(2,1)S(1)}, u32[]{:S(2)}, u32[]{:S(2)}) %all-to-all-start.4) | async-done | bytes 196640 | tf_op jit(solution)/shard_map/all_to_all | solution.py:633
  138.4 0.8 shard_map.122
  (4 shorter events, 0.0 us)
Async XLA Ops:
  4.4 26.2 %all-to-all-start = ((bf16[16,192,128]{2,1,0:T(8,128)(2,1)}), bf16[16,192,128]{2,1,0:T(8,128)(2,1)}, u32[]{:S(2)}, u32[]{:S(2)}) async-start(bf16[16,192,128]{2,1,0:T(8,128)(2,1)} %bitcast.20), calls=%async_computation | async-start | bytes 1572864 | tf_op jit(solution)/shard_map/all_to_all | solution.py:633
  13.1 17.6 %copy-start = (bf16[512,128]{1,0:T(8,128)(2,1)S(1)}, bf16[512,128]{1,0:T(8,128)(2,1)}, u32[]{:S(2)}) copy-start(bf16[512,128]{1,0:T(8,128)(2,1)} %gain_ref.3) | copy-start | bytes 393220
  13.1 17.5 %copy-start.1 = (f32[48,128]{1,0:T(8,128)S(1)}, f32[48,128]{1,0:T(8,128)}, u32[]{:S(2)}) copy-start(f32[48,128]{1,0:T(8,128)} %constant.33.clone.weight_ref) | copy-start | bytes 73732
  30.6 9.9 %copy-start.2 = (bf16[2,128,128]{2,1,0:T(8,128)(2,1)S(1)}, bf16[2,128,128]{2,1,0:T(8,128)(2,1)}, u32[]{:S(2)}) copy-start(bf16[2,128,128]{2,1,0:T(8,128)(2,1)} %param.11) | copy-start | bytes 196612
  35.0 24.3 %all-to-all-start.1 = ((bf16[16,192,128]{2,1,0:T(8,128)(2,1)}), bf16[16,192,128]{2,1,0:T(8,128)(2,1)}, u32[]{:S(2)}, u32[]{:S(2)}) async-start(bf16[16,192,128]{2,1,0:T(8,128)(2,1)} %bitcast.19), calls=%async_computation.1 | async-start | bytes 1572864 | tf_op jit(solution)/shard_map/all_to_all | solution.py:633
  65.5 24.3 %all-to-all-start.2 = ((bf16[16,192,128]{2,1,0:T(8,128)(2,1)}), bf16[16,192,128]{2,1,0:T(8,128)(2,1)}, u32[]{:S(2)}, u32[]{:S(2)}) async-start(bf16[16,192,128]{2,1,0:T(8,128)(2,1)} %bitcast.21), calls=%async_computation.2 | async-start | bytes 1572864 | tf_op jit(solution)/shard_map/all_to_all | solution.py:633
  124.7 13.7 %all-to-all-start.4 = ((bf16[16,48,128]{2,1,0:T(8,128)(2,1)}), bf16[16,48,128]{2,1,0:T(8,128)(2,1)S(1)}, u32[]{:S(2)}, u32[]{:S(2)}) async-start(bf16[16,48,128]{2,1,0:T(8,128)(2,1)} %shard_map.121), calls=%async_computation.4 | async-start | bytes 393216 | tf_op jit(solution)/shard_map/all_to_all | solution.py:633

commit v3 on v2

--- a/solution.py
+++ b/solution.py
@@ -249,38 +249,21 @@
     return [(start, size) for start in range(0, slots, size)]
 
 
-class Landing:
-    def __init__(self, slots, spread_ref, array_hbm, array_ref, sems):
-        lats, rows, channels = array_ref.shape
+class Spread:
+    def __init__(self, slots, spread_ref, array_ref):
+        lats, self.rows, channels = array_ref.shape
+        self.slots = slots
         self.halves = slot_halves(slots)
         self.spread_ref = spread_ref.reshape(lats, spread_ref.shape[0] // lats, channels)
         self.array_ref = array_ref
-        self.copies = {}
-        for half, (start, size) in enumerate(self.halves):
-            group = []
-            for part in range(2):
-                span = slice(part * slots + start, part * slots + start + size)
-                if len(self.halves) == 1:
-                    span = slice(0, rows)
-                for piece in range(2):
-                    block = slice(piece * lats // 2, (piece + 1) * lats // 2)
-                    copy = pltpu.make_async_copy(
-                        array_hbm.at[block, span, :],
-                        array_ref.at[block, span, :],
-                        sems.at[4 * half + 2 * part + piece],
-                    )
-                    group.append((copy, block, span))
-                if len(self.halves) == 1:
-                    break
-            self.copies[start] = group
-        for group in self.copies.values():
-            for copy, _, _ in group:
-                copy.start()
 
     def need(self, slot):
-        for copy, block, span in self.copies.pop(slot, ()):
-            copy.wait()
-            self.spread_ref[block, span, :] = self.array_ref[block, span, :].astype(F32)
+        for start, size in self.halves:
+            if slot == start:
+                for part in range(2):
+                    begin = part * self.slots + start
+                    span = slice(begin, begin + size)
+                    self.spread_ref[:, span, :] = self.array_ref[:, span, :].astype(F32)
 
 
 def staggered(count, delay, first_stage, second_stage):
@@ -295,24 +278,29 @@
 
 def spectrum_kernel(
     devices,
+    modes_ref,
     rows_ref,
-    columns_ref,
     gain_ref,
     weight_ref,
     alpha_ref,
-    modes_hbm,
+    place_ref,
+    columns_hbm,
     out_hbm,
-    modes_ref,
+    columns_ref,
     in_s,
     out_s,
     out_ref,
-    sems,
+    columns_sem,
     out_sems,
 ):
+    columns_copy = pltpu.make_async_copy(
+        columns_hbm.at[place_ref[0]], columns_ref, columns_sem.at[0]
+    )
+    columns_copy.start()
     slots = MODES // devices
     lats = weight_ref.shape[0]
     firsts, offsets, _ = degree_starts(devices)
-    landing = Landing(slots, in_s, modes_hbm, modes_ref, sems)
+    landing = Spread(slots, in_s, modes_ref)
     stores = []
     gain = gain_ref[...]
     channels = gain.shape[1]
@@ -327,6 +315,8 @@
 
     def back(slot, scaled):
         first, offset = firsts[slot], offsets[slot]
+        if slot == 0:
+            columns_copy.wait()
         result = dot(columns_ref[:, offset : offset + MODES - first], scaled)
         result = result * (alpha_ref[...] if slot == 0 else 2.0)
         for part in range(2):
@@ -358,10 +348,10 @@
         copy.wait()
 
 
-def pairs_kernel(devices, weight_ref, modes_hbm, out_ref, modes_ref, in_s, sems):
+def pairs_kernel(devices, weight_ref, modes_ref, out_ref, in_s):
     slots = MODES // devices
     lats = weight_ref.shape[0]
-    landing = Landing(slots, in_s, modes_hbm, modes_ref, sems)
+    landing = Spread(slots, in_s, modes_ref)
     lat_weight = weight_ref[...]
     for slot in range(slots):
         landing.need(slot)
@@ -372,22 +362,22 @@
 
 def gradient_kernel(
     devices,
-    pairs_ref,
+    grads_ref,
     rows_ref,
     gain_ref,
     weight_ref,
     alpha_ref,
     part_ref,
     place_ref,
-    grads_hbm,
+    pairs_hbm,
     columns_hbm,
     out_ref,
     filter_ref,
-    grads_ref,
+    pairs_ref,
     columns_ref,
     grad_s,
     out_s,
-    sems,
+    pairs_sems,
     columns_sem,
 ):
     slots = MODES // devices
@@ -396,8 +386,15 @@
     columns_copy = pltpu.make_async_copy(
         columns_hbm.at[place_ref[0]], columns_ref, columns_sem.at[0]
     )
-    landing = Landing(slots, grad_s, grads_hbm, grads_ref, sems)
-    columns_copy.start()
+    pairs_copies = {}
+    for index, (start, size) in enumerate(slot_halves(slots)):
+        span = slice(start * lats, (start + size) * lats)
+        pairs_copies[start] = pltpu.make_async_copy(
+            pairs_hbm.at[span, :], pairs_ref.at[span, :], pairs_sems.at[index]
+        )
+    for copy in [*pairs_copies.values(), columns_copy]:
+        copy.start()
+    landing = Spread(slots, grad_s, grads_ref)
     gain = gain_ref[...].astype(F32)
     lat_weight = weight_ref[...]
     channels = gain.shape[1]
@@ -406,6 +403,8 @@
     def forward(slot):
         first, offset = firsts[slot], offsets[slot]
         landing.need(slot)
+        if slot in pairs_copies:
+            pairs_copies[slot].wait()
         scale = alpha_ref[:, :channels] if slot == 0 else 2.0
         modes = pairs_ref[slot * lats : (slot + 1) * lats, :]
         grads = slot_pair(grad_s, slot, slots, lats, scale)
@@ -442,20 +441,20 @@
 
 def slope_kernel(
     slots,
+    modes_ref,
     wide_ref,
     wide_t_ref,
-    upstream_ref,
     rows_ref,
-    modes_hbm,
+    upstream_hbm,
     columns_hbm,
     out_hbm,
     weight_ref,
-    modes_ref,
+    upstream_ref,
     columns_ref,
     modes_s,
     folded_s,
     out_ref,
-    sems,
+    upstream_sems,
     columns_sems,
     out_sems,
 ):
@@ -472,17 +471,19 @@
         )
 
     places = [(parity, lat) for parity in range(2) for lat in range(lats)]
-    modes_copies = [lat_copy(modes_hbm, modes_ref, sems, *place) for place in places]
+    upstream_copies = [
+        pltpu.make_async_copy(upstream_hbm.at[lat], upstream_ref.at[lat], upstream_sems.at[lat])
+        for lat in range(lats)
+    ]
     columns_copies = [
         pltpu.make_async_copy(
             columns_hbm.at[parity], columns_ref.at[parity], columns_sems.at[parity]
         )
         for parity in range(2)
     ]
-    for copy in modes_copies + columns_copies:
+    for copy in upstream_copies + columns_copies:
         copy.start()
-    for (parity, lat), copy in zip(places, modes_copies):
-        copy.wait()
+    for parity, lat in places:
         mixed = dot(load_pair(modes_ref, slots, parity, lat), wide_ref[...]).astype(BF16)
         for part in range(2):
             modes_s[
@@ -490,6 +491,8 @@
                 part * block : (part + 1) * block,
                 lat * channels : (lat + 1) * channels,
             ] = mixed[:, part * channels : (part + 1) * channels]
+    for copy in upstream_copies:
+        copy.wait()
     for start, size in row_chunks(half):
         even = dot(rows_ref[0, start : start + size, :], modes_s[0])
         odd = dot(rows_ref[1, start : start + size, :], modes_s[1])
@@ -652,10 +655,14 @@
     half = lon_count // 2
     dft_rows, dft_columns = (jnp.asarray(t) for t in fourier_constant(devices, lon_count))
     constants = table_constants(devices, lat_count)
+    place = me.reshape(1)
     if constants is None:
-        leg_tables = made = made_tables(devices, lat_count, me)
+        leg_rows, leg_columns = made_tables(devices, lat_count, me)
+        leg_columns = leg_columns[None]
+        place = jnp.zeros_like(place)
     else:
-        leg_tables = [lax.dynamic_index_in_dim(t, me, 0, keepdims=False) for t in constants]
+        leg_rows = lax.dynamic_index_in_dim(constants[0], me, 0, keepdims=False)
+        leg_columns = constants[1]
     angles = np.pi * (np.arange(lat_count) + 0.5) / lat_count
     lat_weight = jnp.asarray(
         np.broadcast_to((np.pi / lat_count * np.sin(angles))[:, None], (lat_count, channels)), F32
@@ -673,7 +680,7 @@
     dft_flops = 2 * MODES * lon_count * lats * channels
     leg_flops = 4 * degree_starts(devices)[2] * lat_count * channels
     modes_landing = pltpu.VMEM(mode_shape.shape, BF16)
-    block_sems = pltpu.SemaphoreType.DMA((8,))
+    columns_landing = pltpu.VMEM(leg_columns.shape[1:], BF16)
     weight_rows = 2 * channels // devices
     extra = MODES // devices + weight_rows
     joined = (MODES // devices) % 16 == 0 and weight_rows % 16 == 0
@@ -691,34 +698,31 @@
         [],
         [grid_in, dft_columns],
     )
-    held_upstream, held_rows = (
-        held(
-            call(
-                fetch_kernel,
-                pltpu.VMEM(array.shape, array.dtype),
-                [pltpu.SemaphoreType.DMA((1,))],
-                0,
-                [],
-                [array],
-            )
-        )
-        for array in (upstream, dft_rows)
+    held_rows = held(
+        call(
+            fetch_kernel,
+            pltpu.VMEM(dft_rows.shape, BF16),
+            [pltpu.SemaphoreType.DMA((1,))],
+            0,
+            [],
+            [dft_rows],
+        )
     )
     modes = exchange(fourier.reshape(block_shape)).reshape(mode_shape.shape)
     returned = call(
         functools.partial(spectrum_kernel, devices),
         pltpu.HBM(mode_shape.shape, BF16),
         [
-            modes_landing,
+            columns_landing,
             spread_shape,
             spread_shape,
             modes_landing,
-            block_sems,
+            pltpu.SemaphoreType.DMA((1,)),
             pltpu.SemaphoreType.DMA((4,)),
         ],
         2 * leg_flops,
-        [*(held(table) for table in leg_tables), degree_filter, lat_weight, alpha],
-        [modes],
+        [held(modes), held(leg_rows), degree_filter, lat_weight, alpha, place],
+        [leg_columns],
         written=1,
     )
     returned = exchange(returned.reshape(block_shape)).reshape(grid_shape.shape)
@@ -727,42 +731,37 @@
         functools.partial(slope_kernel, slots),
         [grid_out, jax.ShapeDtypeStruct((2 * channels, channels), F32)],
         [
-            grid_landing,
+            pltpu.VMEM(upstream.shape, BF16),
             pltpu.VMEM(dft_columns.shape, BF16),
             modes_scratch,
             folded_scratch,
             grid_landing,
-            pltpu.SemaphoreType.DMA((2 * lats,)),
+            pltpu.SemaphoreType.DMA((lats,)),
             pltpu.SemaphoreType.DMA((2,)),
             pltpu.SemaphoreType.DMA((2 * lats,)),
         ],
         2 * dft_flops,
-        [wide, wide.T, held_upstream, held_rows],
-        [returned, dft_columns],
+        [held(returned), wide, wide.T, held_rows],
+        [upstream, dft_columns],
         written=1,
     )
-    late_place, mixed_grad = lax.optimization_barrier((me.reshape(1), mixed_grad))
-    if constants is None:
-        late_rows, late_columns = made[0], made[1][None]
-        late_place = jnp.zeros_like(late_place)
-    else:
-        late_columns = constants[1]
+    late_place, late_modes, mixed_grad = lax.optimization_barrier((place, modes, mixed_grad))
+    late_rows = leg_rows
+    if constants is not None:
         late_rows = call(
             fetch_place_kernel,
-            pltpu.VMEM(constants[0].shape[1:], BF16),
+            pltpu.VMEM(leg_rows.shape, BF16),
             [pltpu.SemaphoreType.DMA((1,))],
             0,
             [late_place],
             [constants[0]],
         )
-    late_modes, mixed_grad = lax.optimization_barrier((modes, mixed_grad))
     pairs = call(
         functools.partial(pairs_kernel, devices),
-        pltpu.VMEM((lat_count * slots, 2 * channels), BF16),
-        [modes_landing, spread_shape, block_sems],
+        pltpu.HBM((lat_count * slots, 2 * channels), BF16),
+        [spread_shape],
         0,
-        [lat_weight],
-        [late_modes],
+        [lat_weight, away(late_modes)],
     )
     grads = exchange(mixed_grad.reshape(block_shape)).reshape(mode_shape.shape)
     gfield, filter_part = call(
@@ -772,16 +771,16 @@
             jax.ShapeDtypeStruct((MODES, channels), F32),
         ],
         [
-            modes_landing,
-            pltpu.VMEM(late_columns.shape[1:], BF16),
+            pltpu.VMEM(pairs.shape, BF16),
+            columns_landing,
             spread_shape,
             spread_shape,
-            block_sems,
+            pltpu.SemaphoreType.DMA((2,)),
             pltpu.SemaphoreType.DMA((1,)),
         ],
         3 * leg_flops,
         [
-            held(pairs),
+            held(grads),
             held(late_rows),
             degree_filter,
             lat_weight,
@@ -789,7 +788,7 @@
             weight_part,
             late_place,
         ],
-        [grads, late_columns],
+        [pairs, leg_columns],
     )
     gfield = exchange(gfield)
     if joined:

time: 140 us -> 139 us (level)
    pallas_call x11 -> x10, Pallas kernels: 30.4 us -> 29.2 us  [call(): pl.pallas_call(kernel, out_shape=out_shape, in_specs=[pl.BlockSpec(memory...]
    squeeze x2 -> x1, local copies, waits for them, and re-layouts: 2.91 us -> 1.71 us  [body(): leg_rows = lax.dynamic_index_in_dim(constants[0], me, 0, keepdims=False)]
where the time goes in v3:
time: 139 us; the launch traced here: 138 us
  waiting for transfers between devices  53.8 us (39%)
  Pallas kernels  29.2 us (21%)
  blocking collectives  29 us (21%)
  starting transfers between devices  23.1 us (17%)
  local copies, waits for them, and re-layouts  2.07 us (1%)
    all_to_all x4, waiting for transfers between devices, exchange(): lax.all_to_all(array, 'space', split_axis=0, concat_axis=0, tiled=True)  53.8 us
    pallas_call x10, Pallas kernels, call(): pl.pallas_call(kernel, out_shape=out_shape, in_specs=[pl.BlockSpec(memory...  29.2 us
    all_to_all x1, blocking collectives, exchange(): lax.all_to_all(array, 'space', split_axis=0, concat_axis=0, tiled=True)  29 us
    all_to_all x4, starting transfers between devices, exchange(): lax.all_to_all(array, 'space', split_axis=0, concat_axis=0, tiled=True)  23.1 us
  transfers between devices with their start and end apart: 4, of which 4 were waited for; matrix products, arithmetic and copies ran while one was open for 2% of the time, Pallas kernels for 7%

profile of v3, /device:TPU:0, one launch (start us, length us, event | category | flops | bytes accessed | tf_op | source)
XLA Modules:
  0.0 138.0 jit_solution(3012253125240258518)
XLA Ops:
  0.6 3.8 %shard_map.112 = bf16[8,2,192,128]{3,2,1,0:T(8,128)(2,1)} custom-call(bf16[3,1440,128]{2,1,0:T(8,128)(2,1)} %grid_hbm.1, bf16[2,512,720]{2,1,0:T(8,128)(2,1)} %constant.26.clone.columns_hbm), custom_call_target="tpu_custom_call" | custom-call | flops 566231040 | bytes 3366912 | tf_op jit(solution)/shard_map/pallas_call | solution.py:612
  4.4 7.4 %all-to-all-start = ((bf16[16,192,128]{2,1,0:T(8,128)(2,1)}), bf16[16,192,128]{2,1,0:T(8,128)(2,1)S(1)}, u32[]{:S(2)}, u32[]{:S(2)}) async-start(bf16[16,192,128]{2,1,0:T(8,128)(2,1)} %bitcast.22), calls=%async_computation | async-start | bytes 1572864 | tf_op jit(solution)/shard_map/all_to_all | solution.py:636
  11.8 0.0 copy-start.1
  11.8 0.0 copy-start.2
  11.8 1.7 %dynamic-slice_bitcast_fusion.rows_ref = bf16[8448,48]{1,0:T(8,128)(2,1)S(1)} fusion(bf16[16,8448,48]{2,1,0:T(8,128)(2,1)} %constant.27.clone.source_hbm, s32[]{:T(128)S(6)} %select_n.8), kind=kLoop, calls=%fused_computation | loop fusion | bytes 1622020 | tf_op jit(solution)/shard_map/jit(dynamic_index_in_dim)/squeeze | solution.py:664
  13.6 17.0 %all-to-all-done = bf16[16,192,128]{2,1,0:T(8,128)(2,1)S(1)} async-done(((bf16[16,192,128]{2,1,0:T(8,128)(2,1)}), bf16[16,192,128]{2,1,0:T(8,128)(2,1)S(1)}, u32[]{:S(2)}, u32[]{:S(2)}) %all-to-all-start) | async-done | bytes 786464 | tf_op jit(solution)/shard_map/all_to_all | solution.py:636
  30.5 0.0 copy-start
  30.5 0.0 copy-done.1
  30.5 0.0 copy-done.2
  30.5 0.0 copy-start.3
  30.5 4.1 %shard_map.113 = bf16[48,64,128]{2,1,0:T(8,128)(2,1)} custom-call(bf16[48,64,128]{2,1,0:T(8,128)(2,1)S(1)} %bitcast.17, bf16[8448,48]{1,0:T(8,128)(2,1)S(1)} %dynamic-slice_bitcast_fusion.rows_ref, bf16[512,128]{1,0:T(8,128)(2,1)S(1)} %copy-done.1, f32[48,128]{1,0:T(8,128)S(1)} %copy-done.2, f32[1,256]{1,0:T(1,128)S(1)} %mul.3.alpha_ref, s32[1]{0:T(128)} %bitcast.place_ref, ...), custom_call_target="tpu_custom_call" | custom-call | flops 415236096 | bytes 15503874 | tf_op jit(solution)/shard_map/pallas_call | solution.py:612
  34.6 0.0 copy-done
  34.7 5.5 %all-to-all-start.1 = ((bf16[16,192,128]{2,1,0:T(8,128)(2,1)}), bf16[16,192,128]{2,1,0:T(8,128)(2,1)S(1)}, u32[]{:S(2)}, u32[]{:S(2)}) async-start(bf16[16,192,128]{2,1,0:T(8,128)(2,1)} %bitcast.21), calls=%async_computation.1 | async-start | bytes 1572864 | tf_op jit(solution)/shard_map/all_to_all | solution.py:636
  40.2 0.0 copy-done.3
  40.2 0.1 copy.16
  40.3 0.1 copy.15
  40.5 0.1 copy.14.wide_ref
  40.6 1.4 %shard_map.114.rows_ref = bf16[2,720,512]{2,1,0:T(8,128)(2,1)S(1)} custom-call(bf16[2,720,512]{2,1,0:T(8,128)(2,1)} %constant.25.clone.refs_0_.rows_hbm), custom_call_target="tpu_custom_call" | custom-call | bytes 2949120 | tf_op jit(solution)/shard_map/pallas_call | solution.py:612
  42.0 16.9 %all-to-all-done.1 = bf16[16,192,128]{2,1,0:T(8,128)(2,1)S(1)} async-done(((bf16[16,192,128]{2,1,0:T(8,128)(2,1)}), bf16[16,192,128]{2,1,0:T(8,128)(2,1)S(1)}, u32[]{:S(2)}, u32[]{:S(2)}) %all-to-all-start.1) | async-done | bytes 786464 | tf_op jit(solution)/shard_map/all_to_all | solution.py:636
  58.9 5.6 %shard_map.115 = (bf16[8,2,192,128]{3,2,1,0:T(8,128)(2,1)}, f32[256,128]{1,0:T(8,128)S(1)}) custom-call(bf16[8,2,192,128]{3,2,1,0:T(8,128)(2,1)S(1)} %bitcast.20, bf16[256,256]{1,0:T(8,128)(2,1)S(1)} %copy.14.wide_ref, bf16[256,256]{1,0:T(8,128)(2,1)S(1)} %get-tuple-element.19.wide_t_ref, bf16[2,720,512]{2,1,0:T(8,128)(2,1)S(1)} %shard_map.114.rows_ref, ...), custom_call_target="tpu_custom_call" | custom-call | flops 1132462080 | bytes 5955584 | tf_op jit(solution)/shard_map/pallas_call | solution.py:612
  64.5 5.5 %all-to-all-start.2 = ((bf16[16,192,128]{2,1,0:T(8,128)(2,1)}), bf16[16,192,128]{2,1,0:T(8,128)(2,1)S(1)}, u32[]{:S(2)}, u32[]{:S(2)}) async-start(bf16[16,192,128]{2,1,0:T(8,128)(2,1)} %bitcast.23), calls=%async_computation.2 | async-start | bytes 1572864 | tf_op jit(solution)/shard_map/all_to_all | solution.py:636
  70.0 1.6 %shard_map.116.rows_ref = bf16[8448,48]{1,0:T(8,128)(2,1)S(1)} custom-call(s32[1]{0:T(128)} %bitcast.place_ref, bf16[16,8448,48]{2,1,0:T(8,128)(2,1)} %constant.27.clone.source_hbm), custom_call_target="tpu_custom_call" | custom-call | bytes 13787138 | tf_op jit(solution)/shard_map/pallas_call | solution.py:612
  71.6 2.4 %shard_map.117.pairs_hbm = bf16[1536,256]{1,0:T(8,128)(2,1)} custom-call(f32[48,128]{1,0:T(8,128)S(1)} %copy-done.2, bf16[48,64,128]{2,1,0:T(8,128)(2,1)} %bitcast.18), custom_call_target="tpu_custom_call" | custom-call | bytes 1585152 | tf_op jit(solution)/shard_map/pallas_call | solution.py:612
  74.0 14.7 %all-to-all-done.2 = bf16[16,192,128]{2,1,0:T(8,128)(2,1)S(1)} async-done(((bf16[16,192,128]{2,1,0:T(8,128)(2,1)}), bf16[16,192,128]{2,1,0:T(8,128)(2,1)S(1)}, u32[]{:S(2)}, u32[]{:S(2)}) %all-to-all-start.2) | async-done | bytes 786464 | tf_op jit(solution)/shard_map/all_to_all | solution.py:636
  88.7 5.1 %shard_map.118 = (bf16[16,240,128]{2,1,0:T(8,128)(2,1)S(1)}, f32[512,128]{1,0:T(8,128)}) custom-call(bf16[48,64,128]{2,1,0:T(8,128)(2,1)S(1)} %bitcast.19, bf16[8448,48]{1,0:T(8,128)(2,1)S(1)} %shard_map.116.rows_ref, bf16[512,128]{1,0:T(8,128)(2,1)S(1)} %copy-done.1, f32[48,128]{1,0:T(8,128)S(1)} %copy-done.2, f32[1,256]{1,0:T(1,128)S(1)} %mul.3.alpha_ref, ...), custom_call_target="tpu_custom_call" | custom-call | flops 622854144 | bytes 16683522 | tf_op jit(solution)/shard_map/pallas_call | solution.py:612
  93.8 29.0 %all_to_all.25.received_ref = bf16[16,240,128]{2,1,0:T(8,128)(2,1)S(1)} all-to-all(bf16[16,240,128]{2,1,0:T(8,128)(2,1)S(1)} %get-tuple-element.16), channel_id=1, replica_groups=mesh['groups'=2,'space'=16] {'space'}, dimensions={0} | all-to-all | bytes 1966080 | tf_op jit(solution)/shard_map/all_to_all | solution.py:636
  122.8 0.7 shard_map.120
  123.5 4.7 %all-to-all-start.4 = ((bf16[16,48,128]{2,1,0:T(8,128)(2,1)}), bf16[16,48,128]{2,1,0:T(8,128)(2,1)S(1)}, u32[]{:S(2)}, u32[]{:S(2)}) async-start(bf16[16,48,128]{2,1,0:T(8,128)(2,1)} %shard_map.120), calls=%async_computation.4 | async-start | bytes 393216 | tf_op jit(solution)/shard_map/all_to_all | solution.py:636
  128.2 3.7 %shard_map.119 = bf16[3,1440,128]{2,1,0:T(8,128)(2,1)} custom-call(bf16[8,2,240,128]{3,2,1,0:T(8,128)(2,1)S(1)} %bitcast.16, bf16[3,1440,128]{2,1,0:T(8,128)(2,1)} %upstream_hbm.3, bf16[2,720,512]{2,1,0:T(8,128)(2,1)} %constant.25.clone.refs_0_.rows_hbm), custom_call_target="tpu_custom_call" | custom-call | flops 566231040 | bytes 4669440 | tf_op jit(solution)/shard_map/pallas_call | solution.py:612
  131.9 5.3 %all-to-all-done.4.received_ref = bf16[16,48,128]{2,1,0:T(8,128)(2,1)S(1)} async-done(((bf16[16,48,128]{2,1,0:T(8,128)(2,1)}), bf16[16,48,128]{2,1,0:T(8,128)(2,1)S(1)}, u32[]{:S(2)}, u32[]{:S(2)}) %all-to-all-start.4) | async-done | bytes 196640 | tf_op jit(solution)/shard_map/all_to_all | solution.py:636
  137.2 0.8 shard_map.121
  (4 shorter events, 0.0 us)
Async XLA Ops:
  4.4 26.1 %all-to-all-start = ((bf16[16,192,128]{2,1,0:T(8,128)(2,1)}), bf16[16,192,128]{2,1,0:T(8,128)(2,1)S(1)}, u32[]{:S(2)}, u32[]{:S(2)}) async-start(bf16[16,192,128]{2,1,0:T(8,128)(2,1)} %bitcast.22), calls=%async_computation | async-start | bytes 1572864 | tf_op jit(solution)/shard_map/all_to_all | solution.py:636
  11.8 18.7 %copy-start.1 = (bf16[512,128]{1,0:T(8,128)(2,1)S(1)}, bf16[512,128]{1,0:T(8,128)(2,1)}, u32[]{:S(2)}) copy-start(bf16[512,128]{1,0:T(8,128)(2,1)} %gain_ref.3) | copy-start | bytes 393220
  11.8 18.7 %copy-start.2 = (f32[48,128]{1,0:T(8,128)S(1)}, f32[48,128]{1,0:T(8,128)}, u32[]{:S(2)}) copy-start(f32[48,128]{1,0:T(8,128)} %constant.29.clone.weight_ref) | copy-start | bytes 73732
  30.5 4.1 %copy-start = (bf16[16,192,128]{2,1,0:T(8,128)(2,1)}, bf16[16,192,128]{2,1,0:T(8,128)(2,1)S(1)}, u32[]{:S(2)}) copy-start(bf16[16,192,128]{2,1,0:T(8,128)(2,1)S(1)} %all-to-all-done) | copy-start | bytes 2359300
  30.5 9.6 %copy-start.3 = (bf16[2,128,128]{2,1,0:T(8,128)(2,1)S(1)}, bf16[2,128,128]{2,1,0:T(8,128)(2,1)}, u32[]{:S(2)}) copy-start(bf16[2,128,128]{2,1,0:T(8,128)(2,1)} %param.11) | copy-start | bytes 196612
  34.7 24.2 %all-to-all-start.1 = ((bf16[16,192,128]{2,1,0:T(8,128)(2,1)}), bf16[16,192,128]{2,1,0:T(8,128)(2,1)S(1)}, u32[]{:S(2)}, u32[]{:S(2)}) async-start(bf16[16,192,128]{2,1,0:T(8,128)(2,1)} %bitcast.21), calls=%async_computation.1 | async-start | bytes 1572864 | tf_op jit(solution)/shard_map/all_to_all | solution.py:636
  64.5 24.2 %all-to-all-start.2 = ((bf16[16,192,128]{2,1,0:T(8,128)(2,1)}), bf16[16,192,128]{2,1,0:T(8,128)(2,1)S(1)}, u32[]{:S(2)}, u32[]{:S(2)}) async-start(bf16[16,192,128]{2,1,0:T(8,128)(2,1)} %bitcast.23), calls=%async_computation.2 | async-start | bytes 1572864 | tf_op jit(solution)/shard_map/all_to_all | solution.py:636
  123.5 13.7 %all-to-all-start.4 = ((bf16[16,48,128]{2,1,0:T(8,128)(2,1)}), bf16[16,48,128]{2,1,0:T(8,128)(2,1)S(1)}, u32[]{:S(2)}, u32[]{:S(2)}) async-start(bf16[16,48,128]{2,1,0:T(8,128)(2,1)} %shard_map.120), calls=%async_computation.4 | async-start | bytes 393216 | tf_op jit(solution)/shard_map/all_to_all | solution.py:636

commit v4 on v3

--- a/solution.py
+++ b/solution.py
@@ -13,7 +13,7 @@
 MODES = 512
 TABLE_BYTES = 64 * 1024 * 1024
 VMEM_BYTES = 18 * 1024 * 1024
-DELAY = 4
+DELAY = 7
 BF16 = jnp.bfloat16
 F32 = jnp.float32
 
@@ -191,7 +191,9 @@
 
 
 def fetch_place_kernel(place_ref, source_hbm, out_ref, sems):
-    copy = pltpu.make_async_copy(source_hbm.at[place_ref[0]], out_ref, sems.at[0])
+    copy = pltpu.make_async_copy(
+        source_hbm.at[place_ref[0], : out_ref.shape[0], :], out_ref, sems.at[0]
+    )
     copy.start()
     copy.wait()
 
@@ -226,12 +228,12 @@
     for parity in range(2):
         for part in range(2):
             table_copies[2 * parity + part].wait()
-            result = dot(
-                columns_ref[parity, part * block : (part + 1) * block, :], folded_ref[parity]
-            ).astype(BF16)
+        result = dot(columns_ref[parity], folded_ref[parity]).astype(BF16)
+        for part in range(2):
             for lat in range(lats):
                 lanes = slice(lat * channels, (lat + 1) * channels)
-                store_rows(out_ref, slots, parity, lat, part, result[:, lanes])
+                rows = slice(part * block, (part + 1) * block)
+                store_rows(out_ref, slots, parity, lat, part, result[rows, lanes])
 
 
 def slot_rows(ref, part, slot, slots, lats):
@@ -348,36 +350,42 @@
         copy.wait()
 
 
-def pairs_kernel(devices, weight_ref, modes_ref, out_ref, in_s):
+def pairs_kernel(devices, weight_ref, modes_ref, near_ref, far_ref, in_s):
     slots = MODES // devices
     lats = weight_ref.shape[0]
     landing = Spread(slots, in_s, modes_ref)
     lat_weight = weight_ref[...]
+    near = near_ref.shape[0] // lats
     for slot in range(slots):
         landing.need(slot)
-        out_ref[slot * lats : (slot + 1) * lats, :] = slot_pair(
-            in_s, slot, slots, lats, lat_weight
-        )
+        pair = slot_pair(in_s, slot, slots, lats, lat_weight)
+        if slot < near:
+            near_ref[slot * lats : (slot + 1) * lats, :] = pair
+        else:
+            far_ref[(slot - near) * lats : (slot - near + 1) * lats, :] = pair
 
 
 def gradient_kernel(
     devices,
     grads_ref,
-    rows_ref,
+    near_rows_ref,
+    near_pairs_ref,
     gain_ref,
     weight_ref,
     alpha_ref,
     part_ref,
     place_ref,
-    pairs_hbm,
+    far_pairs_hbm,
+    rows_hbm,
     columns_hbm,
     out_ref,
     filter_ref,
-    pairs_ref,
+    far_pairs_ref,
+    far_rows_ref,
     columns_ref,
     grad_s,
     out_s,
-    pairs_sems,
+    far_sems,
     columns_sem,
 ):
     slots = MODES // devices
@@ -386,13 +394,15 @@
     columns_copy = pltpu.make_async_copy(
         columns_hbm.at[place_ref[0]], columns_ref, columns_sem.at[0]
     )
-    pairs_copies = {}
-    for index, (start, size) in enumerate(slot_halves(slots)):
-        span = slice(start * lats, (start + size) * lats)
-        pairs_copies[start] = pltpu.make_async_copy(
-            pairs_hbm.at[span, :], pairs_ref.at[span, :], pairs_sems.at[index]
-        )
-    for copy in [*pairs_copies.values(), columns_copy]:
+    near = near_pairs_ref.shape[0] // lats
+    split = near_rows_ref.shape[0]
+    far_copies = [
+        pltpu.make_async_copy(far_pairs_hbm, far_pairs_ref, far_sems.at[0]),
+        pltpu.make_async_copy(
+            rows_hbm.at[place_ref[0], split:, :], far_rows_ref, far_sems.at[1]
+        ),
+    ]
+    for copy in [columns_copy, *far_copies]:
         copy.start()
     landing = Spread(slots, grad_s, grads_ref)
     gain = gain_ref[...].astype(F32)
@@ -403,10 +413,16 @@
     def forward(slot):
         first, offset = firsts[slot], offsets[slot]
         landing.need(slot)
-        if slot in pairs_copies:
-            pairs_copies[slot].wait()
+        if slot == near:
+            for copy in far_copies:
+                copy.wait()
         scale = alpha_ref[:, :channels] if slot == 0 else 2.0
-        modes = pairs_ref[slot * lats : (slot + 1) * lats, :]
+        pairs_ref, rows_ref = near_pairs_ref, near_rows_ref
+        place = slot
+        if slot >= near:
+            pairs_ref, rows_ref = far_pairs_ref, far_rows_ref
+            place, offset = slot - near, offset - split
+        modes = pairs_ref[place * lats : (place + 1) * lats, :]
         grads = slot_pair(grad_s, slot, slots, lats, scale)
         table = rows_ref[offset : offset + MODES - first, :]
         spectrum = dot(table, modes)
@@ -444,17 +460,18 @@
     modes_ref,
     wide_ref,
     wide_t_ref,
-    rows_ref,
-    upstream_hbm,
+    upstream_ref,
+    first_ref,
+    rows_hbm,
     columns_hbm,
     out_hbm,
     weight_ref,
-    upstream_ref,
+    rows_ref,
     columns_ref,
     modes_s,
     folded_s,
     out_ref,
-    upstream_sems,
+    rows_sems,
     columns_sems,
     out_sems,
 ):
@@ -471,9 +488,17 @@
         )
 
     places = [(parity, lat) for parity in range(2) for lat in range(lats)]
-    upstream_copies = [
-        pltpu.make_async_copy(upstream_hbm.at[lat], upstream_ref.at[lat], upstream_sems.at[lat])
-        for lat in range(lats)
+    rows_copies = [
+        [
+            pltpu.make_async_copy(
+                rows_hbm.at[parity, start : start + size, :],
+                rows_ref.at[parity, start : start + size, :],
+                rows_sems.at[2 * chunk + parity],
+            )
+            for parity in range(2)
+        ]
+        for chunk, (start, size) in enumerate(row_chunks(half))
+        if chunk
     ]
     columns_copies = [
         pltpu.make_async_copy(
@@ -481,21 +506,26 @@
         )
         for parity in range(2)
     ]
-    for copy in upstream_copies + columns_copies:
+    for copy in [*sum(rows_copies, []), *columns_copies]:
         copy.start()
-    for parity, lat in places:
-        mixed = dot(load_pair(modes_ref, slots, parity, lat), wide_ref[...]).astype(BF16)
+    mixed = dot(
+        jnp.concatenate([load_pair(modes_ref, slots, *place) for place in places], 0), wide_ref[...]
+    ).astype(BF16)
+    for index, (parity, lat) in enumerate(places):
         for part in range(2):
             modes_s[
                 parity,
                 part * block : (part + 1) * block,
                 lat * channels : (lat + 1) * channels,
-            ] = mixed[:, part * channels : (part + 1) * channels]
-    for copy in upstream_copies:
-        copy.wait()
-    for start, size in row_chunks(half):
-        even = dot(rows_ref[0, start : start + size, :], modes_s[0])
-        odd = dot(rows_ref[1, start : start + size, :], modes_s[1])
+            ] = mixed[
+                index * block : (index + 1) * block, part * channels : (part + 1) * channels
+            ]
+    for chunk, (start, size) in enumerate(row_chunks(half)):
+        for copy in rows_copies[chunk - 1] if chunk else ():
+            copy.wait()
+        table = rows_ref if chunk else first_ref
+        even = dot(table[0, start : start + size, :], modes_s[0])
+        odd = dot(table[1, start : start + size, :], modes_s[1])
         for lat in range(lats):
             lanes = slice(lat * channels, (lat + 1) * channels)
             near = upstream_ref[lat, start : start + size, :].astype(F32) * gelu_slope(
@@ -509,16 +539,21 @@
     pairs, stores = [], []
     for parity in range(2):
         columns_copies[parity].wait()
-        parts = [
-            dot(
-                columns_ref[parity, part * block : (part + 1) * block, :], folded_s[parity]
-            ).astype(BF16)
-            for part in range(2)
+        raw = dot(columns_ref[parity], folded_s[parity]).astype(BF16)
+        parity_pairs = [
+            jnp.concatenate(
+                [
+                    raw[
+                        part * block : (part + 1) * block, lat * channels : (lat + 1) * channels
+                    ]
+                    for part in range(2)
+                ],
+                1,
+            )
+            for lat in range(lats)
         ]
+        mixed = dot(jnp.concatenate(parity_pairs, 0), wide_t_ref[...]).astype(BF16)
         for lat in range(lats):
-            lanes = slice(lat * channels, (lat + 1) * channels)
-            pair = jnp.concatenate([parts[0][:, lanes], parts[1][:, lanes]], 1)
-            mixed = dot(pair, wide_t_ref[...]).astype(BF16)
             for part in range(2):
                 store_rows(
                     out_ref,
@@ -526,11 +561,13 @@
                     parity,
                     lat,
                     part,
-                    mixed[:, part * channels : (part + 1) * channels],
+                    mixed[
+                        lat * block : (lat + 1) * block, part * channels : (part + 1) * channels
+                    ],
                 )
             stores.append(lat_copy(out_ref, out_hbm, out_sems, parity, lat))
             stores[-1].start()
-            pairs.append(pair)
+        pairs += parity_pairs
     total = jnp.zeros((2 * channels, 2 * channels), F32)
     for (parity, lat), pair in zip(places, pairs):
         total = total + lax.dot_general(
@@ -653,7 +690,9 @@
     lat_count = lats * devices
     slots = MODES // devices
     half = lon_count // 2
-    dft_rows, dft_columns = (jnp.asarray(t) for t in fourier_constant(devices, lon_count))
+    dft_rows, dft_columns = fourier_constant(devices, lon_count)
+    first_rows = jnp.asarray(dft_rows[:, : row_chunks(half)[0][1]])
+    dft_rows, dft_columns = jnp.asarray(dft_rows), jnp.asarray(dft_columns)
     constants = table_constants(devices, lat_count)
     place = me.reshape(1)
     if constants is None:
@@ -698,15 +737,18 @@
         [],
         [grid_in, dft_columns],
     )
-    held_rows = held(
-        call(
-            fetch_kernel,
-            pltpu.VMEM(dft_rows.shape, BF16),
-            [pltpu.SemaphoreType.DMA((1,))],
-            0,
-            [],
-            [dft_rows],
-        )
+    held_upstream, held_first = (
+        held(
+            call(
+                fetch_kernel,
+                pltpu.VMEM(array.shape, BF16),
+                [pltpu.SemaphoreType.DMA((1,))],
+                0,
+                [],
+                [array],
+            )
+        )
+        for array in (upstream, first_rows)
     )
     modes = exchange(fourier.reshape(block_shape)).reshape(mode_shape.shape)
     returned = call(
@@ -731,34 +773,43 @@
         functools.partial(slope_kernel, slots),
         [grid_out, jax.ShapeDtypeStruct((2 * channels, channels), F32)],
         [
-            pltpu.VMEM(upstream.shape, BF16),
+            pltpu.VMEM(dft_rows.shape, BF16),
             pltpu.VMEM(dft_columns.shape, BF16),
             modes_scratch,
             folded_scratch,
             grid_landing,
-            pltpu.SemaphoreType.DMA((lats,)),
+            pltpu.SemaphoreType.DMA((2 * len(row_chunks(half)),)),
             pltpu.SemaphoreType.DMA((2,)),
             pltpu.SemaphoreType.DMA((2 * lats,)),
         ],
         2 * dft_flops,
-        [held(returned), wide, wide.T, held_rows],
-        [upstream, dft_columns],
+        [held(returned), wide, wide.T, held_upstream, held_first],
+        [dft_rows, dft_columns],
         written=1,
     )
     late_place, late_modes, mixed_grad = lax.optimization_barrier((place, modes, mixed_grad))
-    late_rows = leg_rows
+    near = slot_halves(slots)[0][1]
+    if near == slots:
+        near = slots // 2
+    split = degree_starts(devices)[1][near]
+    late_rows, near_rows = leg_rows[None], leg_rows[:split]
     if constants is not None:
-        late_rows = call(
+        late_rows = constants[0]
+        near_rows = call(
             fetch_place_kernel,
-            pltpu.VMEM(leg_rows.shape, BF16),
+            pltpu.VMEM((split, lat_count), BF16),
             [pltpu.SemaphoreType.DMA((1,))],
             0,
             [late_place],
-            [constants[0]],
-        )
-    pairs = call(
+            [late_rows],
+        )
+    far_pairs_shape = ((slots - near) * lat_count, 2 * channels)
+    near_pairs, far_pairs = call(
         functools.partial(pairs_kernel, devices),
-        pltpu.HBM((lat_count * slots, 2 * channels), BF16),
+        [
+            pltpu.VMEM((near * lat_count, 2 * channels), BF16),
+            pltpu.HBM(far_pairs_shape, BF16),
+        ],
         [spread_shape],
         0,
         [lat_weight, away(late_modes)],
@@ -771,7 +822,8 @@
             jax.ShapeDtypeStruct((MODES, channels), F32),
         ],
         [
-            pltpu.VMEM(pairs.shape, BF16),
+            pltpu.VMEM(far_pairs_shape, BF16),
+            pltpu.VMEM((leg_rows.shape[0] - split, lat_count), BF16),
             columns_landing,
             spread_shape,
             spread_shape,
@@ -781,14 +833,15 @@
         3 * leg_flops,
         [
             held(grads),
-            held(late_rows),
+            held(near_rows),
+            held(near_pairs),
             degree_filter,
             lat_weight,
             alpha,
             weight_part,
             late_place,
         ],
-        [pairs, leg_columns],
+        [far_pairs, late_rows, leg_columns],
     )
     gfield = exchange(gfield)
     if joined:

time: 139 us -> 137 us (0.986)
    pallas_call x10 -> x11, Pallas kernels: 29.2 us -> 28.2 us  [call(): pl.pallas_call(kernel, out_shape=out_shape, in_specs=[pl.BlockSpec(memory...]
where the time goes in v4:
time: 137 us
  waiting for transfers between devices  53.3 us (39%)
  blocking collectives  29 us (21%)
  Pallas kernels  28.2 us (21%)
  starting transfers between devices  23.2 us (17%)
  local copies, waits for them, and re-layouts  2.07 us (2%)
    all_to_all x4, waiting for transfers between devices, exchange(): lax.all_to_all(array, 'space', split_axis=0, concat_axis=0, tiled=True)  53.3 us
    all_to_all x1, blocking collectives, exchange(): lax.all_to_all(array, 'space', split_axis=0, concat_axis=0, tiled=True)  29 us
    pallas_call x11, Pallas kernels, call(): pl.pallas_call(kernel, out_shape=out_shape, in_specs=[pl.BlockSpec(memory...  28.2 us
    all_to_all x4, starting transfers between devices, exchange(): lax.all_to_all(array, 'space', split_axis=0, concat_axis=0, tiled=True)  23.2 us
  transfers between devices with their start and end apart: 4, of which 4 were waited for; matrix products, arithmetic and copies ran while one was open for 2% of the time, Pallas kernels for 7%

profile of v4, /device:TPU:0, one launch (start us, length us, event | category | flops | bytes accessed | tf_op | source)
XLA Modules:
  0.0 136.6 jit_solution(17643486023744283800)
XLA Ops:
  0.6 3.5 %shard_map.121 = bf16[8,2,192,128]{3,2,1,0:T(8,128)(2,1)} custom-call(bf16[3,1440,128]{2,1,0:T(8,128)(2,1)} %grid_hbm.1, bf16[2,512,720]{2,1,0:T(8,128)(2,1)} %constant.29.clone.columns_hbm), custom_call_target="tpu_custom_call" | custom-call | flops 566231040 | bytes 3366912 | tf_op jit(solution)/shard_map/pallas_call | solution.py:649
  4.2 7.4 %all-to-all-start = ((bf16[16,192,128]{2,1,0:T(8,128)(2,1)}), bf16[16,192,128]{2,1,0:T(8,128)(2,1)S(1)}, u32[]{:S(2)}, u32[]{:S(2)}) async-start(bf16[16,192,128]{2,1,0:T(8,128)(2,1)} %bitcast.22), calls=%async_computation | async-start | bytes 1572864 | tf_op jit(solution)/shard_map/all_to_all | solution.py:673
  11.6 0.0 copy-start.1
  11.6 0.0 copy-start.2
  11.6 1.7 %dynamic-slice_bitcast_fusion.rows_ref = bf16[8448,48]{1,0:T(8,128)(2,1)S(1)} fusion(bf16[16,8448,48]{2,1,0:T(8,128)(2,1)} %constant.30.clone.source_hbm.rows_hbm, s32[]{:T(128)S(6)} %select_n.8), kind=kLoop, calls=%fused_computation | loop fusion | bytes 1622020 | tf_op jit(solution)/shard_map/jit(dynamic_index_in_dim)/squeeze | solution.py:703
  13.3 17.0 %all-to-all-done = bf16[16,192,128]{2,1,0:T(8,128)(2,1)S(1)} async-done(((bf16[16,192,128]{2,1,0:T(8,128)(2,1)}), bf16[16,192,128]{2,1,0:T(8,128)(2,1)S(1)}, u32[]{:S(2)}, u32[]{:S(2)}) %all-to-all-start) | async-done | bytes 786464 | tf_op jit(solution)/shard_map/all_to_all | solution.py:673
  30.3 0.0 copy-start
  30.3 0.0 copy-done.1
  30.3 0.0 copy-done.2
  30.3 3.9 %shard_map.122 = bf16[48,64,128]{2,1,0:T(8,128)(2,1)} custom-call(bf16[48,64,128]{2,1,0:T(8,128)(2,1)S(1)} %bitcast.17, bf16[8448,48]{1,0:T(8,128)(2,1)S(1)} %dynamic-slice_bitcast_fusion.rows_ref, bf16[512,128]{1,0:T(8,128)(2,1)S(1)} %copy-done.1, f32[48,128]{1,0:T(8,128)S(1)} %copy-done.2, f32[1,256]{1,0:T(1,128)S(1)} %mul.3.alpha_ref, s32[1]{0:T(128)} %bitcast.place_ref, ...), custom_call_target="tpu_custom_call" | custom-call | flops 415236096 | bytes 15503874 | tf_op jit(solution)/shard_map/pallas_call | solution.py:649
  34.2 0.0 copy-done
  34.2 0.0 copy-start.3
  34.2 5.6 %all-to-all-start.1 = ((bf16[16,192,128]{2,1,0:T(8,128)(2,1)}), bf16[16,192,128]{2,1,0:T(8,128)(2,1)S(1)}, u32[]{:S(2)}, u32[]{:S(2)}) async-start(bf16[16,192,128]{2,1,0:T(8,128)(2,1)} %bitcast.21), calls=%async_computation.1 | async-start | bytes 1572864 | tf_op jit(solution)/shard_map/all_to_all | solution.py:673
  39.8 0.0 copy-done.3
  39.8 0.1 copy.17
  40.0 0.1 copy.16
  40.1 0.1 copy.15.wide_ref
  40.2 1.3 shard_map.123.upstream_ref
  41.5 1.0 shard_map.124.first_ref
  42.5 16.0 %all-to-all-done.1 = bf16[16,192,128]{2,1,0:T(8,128)(2,1)S(1)} async-done(((bf16[16,192,128]{2,1,0:T(8,128)(2,1)}), bf16[16,192,128]{2,1,0:T(8,128)(2,1)S(1)}, u32[]{:S(2)}, u32[]{:S(2)}) %all-to-all-start.1) | async-done | bytes 786464 | tf_op jit(solution)/shard_map/all_to_all | solution.py:673
  58.5 5.1 %shard_map.125 = (bf16[8,2,192,128]{3,2,1,0:T(8,128)(2,1)}, f32[256,128]{1,0:T(8,128)S(1)}) custom-call(bf16[8,2,192,128]{3,2,1,0:T(8,128)(2,1)S(1)} %bitcast.19, bf16[256,256]{1,0:T(8,128)(2,1)S(1)} %copy.15.wide_ref, bf16[256,256]{1,0:T(8,128)(2,1)S(1)} %get-tuple-element.23.wide_t_ref, bf16[3,1440,128]{2,1,0:T(8,128)(2,1)S(1)} %shard_map.123.upstream_ref, ...), custom_call_target="tpu_custom_call" | custom-call | flops 1132462080 | bytes 6447104 | tf_op jit(solution)/shard_map/pallas_call | solution.py:649
  63.7 5.5 %all-to-all-start.2 = ((bf16[16,192,128]{2,1,0:T(8,128)(2,1)}), bf16[16,192,128]{2,1,0:T(8,128)(2,1)S(1)}, u32[]{:S(2)}, u32[]{:S(2)}) async-start(bf16[16,192,128]{2,1,0:T(8,128)(2,1)} %bitcast.23), calls=%async_computation.2 | async-start | bytes 1572864 | tf_op jit(solution)/shard_map/all_to_all | solution.py:673
  69.2 1.4 %shard_map.126.near_rows_ref = bf16[6272,48]{1,0:T(8,128)(2,1)S(1)} custom-call(s32[1]{0:T(128)} %bitcast.place_ref, bf16[16,8448,48]{2,1,0:T(8,128)(2,1)} %constant.30.clone.source_hbm.rows_hbm), custom_call_target="tpu_custom_call" | custom-call | bytes 13578242 | tf_op jit(solution)/shard_map/pallas_call | solution.py:649
  70.6 2.2 %shard_map.127 = (bf16[768,256]{1,0:T(8,128)(2,1)S(1)}, bf16[768,256]{1,0:T(8,128)(2,1)}) custom-call(f32[48,128]{1,0:T(8,128)S(1)} %copy-done.2, bf16[48,64,128]{2,1,0:T(8,128)(2,1)} %bitcast.18), custom_call_target="tpu_custom_call" | custom-call | bytes 1585152 | tf_op jit(solution)/shard_map/pallas_call | solution.py:649
  72.8 15.0 %all-to-all-done.2 = bf16[16,192,128]{2,1,0:T(8,128)(2,1)S(1)} async-done(((bf16[16,192,128]{2,1,0:T(8,128)(2,1)}), bf16[16,192,128]{2,1,0:T(8,128)(2,1)S(1)}, u32[]{:S(2)}, u32[]{:S(2)}) %all-to-all-start.2) | async-done | bytes 786464 | tf_op jit(solution)/shard_map/all_to_all | solution.py:673
  87.9 4.5 %shard_map.128 = (bf16[16,240,128]{2,1,0:T(8,128)(2,1)S(1)}, f32[512,128]{1,0:T(8,128)}) custom-call(bf16[48,64,128]{2,1,0:T(8,128)(2,1)S(1)} %bitcast.20, bf16[6272,48]{1,0:T(8,128)(2,1)S(1)} %shard_map.126.near_rows_ref, bf16[768,256]{1,0:T(8,128)(2,1)S(1)} %get-tuple-element.17.near_pairs_ref, bf16[512,128]{1,0:T(8,128)(2,1)S(1)} %copy-done.1, ...), custom_call_target="tpu_custom_call" | custom-call | flops 622854144 | bytes 29450754 | tf_op jit(solution)/shard_map/pallas_call | solution.py:649
  92.4 29.0 %all_to_all.25.received_ref = bf16[16,240,128]{2,1,0:T(8,128)(2,1)S(1)} all-to-all(bf16[16,240,128]{2,1,0:T(8,128)(2,1)S(1)} %get-tuple-element.20), channel_id=1, replica_groups=mesh['groups'=2,'space'=16] {'space'}, dimensions={0} | all-to-all | bytes 1966080 | tf_op jit(solution)/shard_map/all_to_all | solution.py:673
  121.3 0.7 shard_map.130
  122.1 4.7 %all-to-all-start.4 = ((bf16[16,48,128]{2,1,0:T(8,128)(2,1)}), bf16[16,48,128]{2,1,0:T(8,128)(2,1)S(1)}, u32[]{:S(2)}, u32[]{:S(2)}) async-start(bf16[16,48,128]{2,1,0:T(8,128)(2,1)} %shard_map.130), calls=%async_computation.4 | async-start | bytes 393216 | tf_op jit(solution)/shard_map/all_to_all | solution.py:673
  126.8 3.7 %shard_map.129 = bf16[3,1440,128]{2,1,0:T(8,128)(2,1)} custom-call(bf16[8,2,240,128]{3,2,1,0:T(8,128)(2,1)S(1)} %bitcast.16, bf16[3,1440,128]{2,1,0:T(8,128)(2,1)} %upstream_hbm.1, bf16[2,720,512]{2,1,0:T(8,128)(2,1)} %constant.28.clone.rows_hbm), custom_call_target="tpu_custom_call" | custom-call | flops 566231040 | bytes 4669440 | tf_op jit(solution)/shard_map/pallas_call | solution.py:649
  130.5 5.3 %all-to-all-done.4.received_ref = bf16[16,48,128]{2,1,0:T(8,128)(2,1)S(1)} async-done(((bf16[16,48,128]{2,1,0:T(8,128)(2,1)}), bf16[16,48,128]{2,1,0:T(8,128)(2,1)S(1)}, u32[]{:S(2)}, u32[]{:S(2)}) %all-to-all-start.4) | async-done | bytes 196640 | tf_op jit(solution)/shard_map/all_to_all | solution.py:673
  135.8 0.8 shard_map.131
  (4 shorter events, 0.0 us)
Async XLA Ops:
  4.2 26.1 %all-to-all-start = ((bf16[16,192,128]{2,1,0:T(8,128)(2,1)}), bf16[16,192,128]{2,1,0:T(8,128)(2,1)S(1)}, u32[]{:S(2)}, u32[]{:S(2)}) async-start(bf16[16,192,128]{2,1,0:T(8,128)(2,1)} %bitcast.22), calls=%async_computation | async-start | bytes 1572864 | tf_op jit(solution)/shard_map/all_to_all | solution.py:673
  11.6 18.7 %copy-start.1 = (bf16[512,128]{1,0:T(8,128)(2,1)S(1)}, bf16[512,128]{1,0:T(8,128)(2,1)}, u32[]{:S(2)}) copy-start(bf16[512,128]{1,0:T(8,128)(2,1)} %gain_ref.3) | copy-start | bytes 393220
  11.6 18.7 %copy-start.2 = (f32[48,128]{1,0:T(8,128)S(1)}, f32[48,128]{1,0:T(8,128)}, u32[]{:S(2)}) copy-start(f32[48,128]{1,0:T(8,128)} %constant.32.clone.weight_ref) | copy-start | bytes 73732
  30.3 3.9 %copy-start = (bf16[16,192,128]{2,1,0:T(8,128)(2,1)}, bf16[16,192,128]{2,1,0:T(8,128)(2,1)S(1)}, u32[]{:S(2)}) copy-start(bf16[16,192,128]{2,1,0:T(8,128)(2,1)S(1)} %all-to-all-done) | copy-start | bytes 2359300
  34.2 5.6 %copy-start.3 = (bf16[2,128,128]{2,1,0:T(8,128)(2,1)S(1)}, bf16[2,128,128]{2,1,0:T(8,128)(2,1)}, u32[]{:S(2)}) copy-start(bf16[2,128,128]{2,1,0:T(8,128)(2,1)} %param.12) | copy-start | bytes 196612
  34.2 24.3 %all-to-all-start.1 = ((bf16[16,192,128]{2,1,0:T(8,128)(2,1)}), bf16[16,192,128]{2,1,0:T(8,128)(2,1)S(1)}, u32[]{:S(2)}, u32[]{:S(2)}) async-start(bf16[16,192,128]{2,1,0:T(8,128)(2,1)} %bitcast.21), calls=%async_computation.1 | async-start | bytes 1572864 | tf_op jit(solution)/shard_map/all_to_all | solution.py:673
  63.7 24.2 %all-to-all-start.2 = ((bf16[16,192,128]{2,1,0:T(8,128)(2,1)}), bf16[16,192,128]{2,1,0:T(8,128)(2,1)S(1)}, u32[]{:S(2)}, u32[]{:S(2)}) async-start(bf16[16,192,128]{2,1,0:T(8,128)(2,1)} %bitcast.23), calls=%async_computation.2 | async-start | bytes 1572864 | tf_op jit(solution)/shard_map/all_to_all | solution.py:673
  122.1 13.7 %all-to-all-start.4 = ((bf16[16,48,128]{2,1,0:T(8,128)(2,1)}), bf16[16,48,128]{2,1,0:T(8,128)(2,1)S(1)}, u32[]{:S(2)}, u32[]{:S(2)}) async-start(bf16[16,48,128]{2,1,0:T(8,128)(2,1)} %shard_map.130), calls=%async_computation.4 | async-start | bytes 393216 | tf_op jit(solution)/shard_map/all_to_all | solution.py:673

commit v5 on v4

--- a/solution.py
+++ b/solution.py
@@ -13,7 +13,7 @@
 MODES = 512
 TABLE_BYTES = 64 * 1024 * 1024
 VMEM_BYTES = 18 * 1024 * 1024
-DELAY = 7
+DELAY = 12
 BF16 = jnp.bfloat16
 F32 = jnp.float32
 

time: 137 us -> 137 us (level)
  no operation moved by 1% of the time
where the time goes in v5:
time: 137 us; the launch traced here: 136 us
  waiting for transfers between devices  53.3 us (39%)
  blocking collectives  29 us (21%)
  Pallas kernels  27.5 us (20%)
  starting transfers between devices  23.2 us (17%)
  local copies, waits for them, and re-layouts  2.07 us (2%)
    all_to_all x4, waiting for transfers between devices, exchange(): lax.all_to_all(array, 'space', split_axis=0, concat_axis=0, tiled=True)  53.3 us
    all_to_all x1, blocking collectives, exchange(): lax.all_to_all(array, 'space', split_axis=0, concat_axis=0, tiled=True)  29 us
    pallas_call x11, Pallas kernels, call(): pl.pallas_call(kernel, out_shape=out_shape, in_specs=[pl.BlockSpec(memory...  27.5 us
    all_to_all x4, starting transfers between devices, exchange(): lax.all_to_all(array, 'space', split_axis=0, concat_axis=0, tiled=True)  23.2 us
  transfers between devices with their start and end apart: 4, of which 4 were waited for; matrix products, arithmetic and copies ran while one was open for 2% of the time, Pallas kernels for 7%

profile of v5, /device:TPU:0, one launch (start us, length us, event | category | flops | bytes accessed | tf_op | source)
XLA Modules:
  0.0 135.9 jit_solution(3715074695028295289)
XLA Ops:
  0.6 3.5 %shard_map.121 = bf16[8,2,192,128]{3,2,1,0:T(8,128)(2,1)} custom-call(bf16[3,1440,128]{2,1,0:T(8,128)(2,1)} %grid_hbm.1, bf16[2,512,720]{2,1,0:T(8,128)(2,1)} %constant.29.clone.columns_hbm), custom_call_target="tpu_custom_call" | custom-call | flops 566231040 | bytes 3366912 | tf_op jit(solution)/shard_map/pallas_call | solution.py:649
  4.2 7.4 %all-to-all-start = ((bf16[16,192,128]{2,1,0:T(8,128)(2,1)}), bf16[16,192,128]{2,1,0:T(8,128)(2,1)S(1)}, u32[]{:S(2)}, u32[]{:S(2)}) async-start(bf16[16,192,128]{2,1,0:T(8,128)(2,1)} %bitcast.22), calls=%async_computation | async-start | bytes 1572864 | tf_op jit(solution)/shard_map/all_to_all | solution.py:673
  11.6 0.0 copy-start.1
  11.6 0.0 copy-start.2
  11.6 1.7 %dynamic-slice_bitcast_fusion.rows_ref = bf16[8448,48]{1,0:T(8,128)(2,1)S(1)} fusion(bf16[16,8448,48]{2,1,0:T(8,128)(2,1)} %constant.30.clone.source_hbm.rows_hbm, s32[]{:T(128)S(6)} %select_n.8), kind=kLoop, calls=%fused_computation | loop fusion | bytes 1622020 | tf_op jit(solution)/shard_map/jit(dynamic_index_in_dim)/squeeze | solution.py:703
  13.3 17.0 %all-to-all-done = bf16[16,192,128]{2,1,0:T(8,128)(2,1)S(1)} async-done(((bf16[16,192,128]{2,1,0:T(8,128)(2,1)}), bf16[16,192,128]{2,1,0:T(8,128)(2,1)S(1)}, u32[]{:S(2)}, u32[]{:S(2)}) %all-to-all-start) | async-done | bytes 786464 | tf_op jit(solution)/shard_map/all_to_all | solution.py:673
  30.3 0.0 copy-start
  30.3 0.0 copy-done.1
  30.3 0.0 copy-done.2
  30.3 3.6 %shard_map.122 = bf16[48,64,128]{2,1,0:T(8,128)(2,1)} custom-call(bf16[48,64,128]{2,1,0:T(8,128)(2,1)S(1)} %bitcast.17, bf16[8448,48]{1,0:T(8,128)(2,1)S(1)} %dynamic-slice_bitcast_fusion.rows_ref, bf16[512,128]{1,0:T(8,128)(2,1)S(1)} %copy-done.1, f32[48,128]{1,0:T(8,128)S(1)} %copy-done.2, f32[1,256]{1,0:T(1,128)S(1)} %mul.3.alpha_ref, s32[1]{0:T(128)} %bitcast.place_ref, ...), custom_call_target="tpu_custom_call" | custom-call | flops 415236096 | bytes 15503874 | tf_op jit(solution)/shard_map/pallas_call | solution.py:649
  33.9 0.0 copy-done
  33.9 0.0 copy-start.3
  34.0 5.6 %all-to-all-start.1 = ((bf16[16,192,128]{2,1,0:T(8,128)(2,1)}), bf16[16,192,128]{2,1,0:T(8,128)(2,1)S(1)}, u32[]{:S(2)}, u32[]{:S(2)}) async-start(bf16[16,192,128]{2,1,0:T(8,128)(2,1)} %bitcast.21), calls=%async_computation.1 | async-start | bytes 1572864 | tf_op jit(solution)/shard_map/all_to_all | solution.py:673
  39.6 0.0 copy-done.3
  39.6 0.1 copy.17
  39.7 0.1 copy.16
  39.9 0.1 copy.15.wide_ref
  40.0 1.3 shard_map.123.upstream_ref
  41.3 1.0 shard_map.124.first_ref
  42.3 16.0 %all-to-all-done.1 = bf16[16,192,128]{2,1,0:T(8,128)(2,1)S(1)} async-done(((bf16[16,192,128]{2,1,0:T(8,128)(2,1)}), bf16[16,192,128]{2,1,0:T(8,128)(2,1)S(1)}, u32[]{:S(2)}, u32[]{:S(2)}) %all-to-all-start.1) | async-done | bytes 786464 | tf_op jit(solution)/shard_map/all_to_all | solution.py:673
  58.3 5.1 %shard_map.125 = (bf16[8,2,192,128]{3,2,1,0:T(8,128)(2,1)}, f32[256,128]{1,0:T(8,128)S(1)}) custom-call(bf16[8,2,192,128]{3,2,1,0:T(8,128)(2,1)S(1)} %bitcast.19, bf16[256,256]{1,0:T(8,128)(2,1)S(1)} %copy.15.wide_ref, bf16[256,256]{1,0:T(8,128)(2,1)S(1)} %get-tuple-element.23.wide_t_ref, bf16[3,1440,128]{2,1,0:T(8,128)(2,1)S(1)} %shard_map.123.upstream_ref, ...), custom_call_target="tpu_custom_call" | custom-call | flops 1132462080 | bytes 6447104 | tf_op jit(solution)/shard_map/pallas_call | solution.py:649
  63.4 5.5 %all-to-all-start.2 = ((bf16[16,192,128]{2,1,0:T(8,128)(2,1)}), bf16[16,192,128]{2,1,0:T(8,128)(2,1)S(1)}, u32[]{:S(2)}, u32[]{:S(2)}) async-start(bf16[16,192,128]{2,1,0:T(8,128)(2,1)} %bitcast.23), calls=%async_computation.2 | async-start | bytes 1572864 | tf_op jit(solution)/shard_map/all_to_all | solution.py:673
  68.9 1.4 %shard_map.126.near_rows_ref = bf16[6272,48]{1,0:T(8,128)(2,1)S(1)} custom-call(s32[1]{0:T(128)} %bitcast.place_ref, bf16[16,8448,48]{2,1,0:T(8,128)(2,1)} %constant.30.clone.source_hbm.rows_hbm), custom_call_target="tpu_custom_call" | custom-call | bytes 13578242 | tf_op jit(solution)/shard_map/pallas_call | solution.py:649
  70.4 2.2 %shard_map.127 = (bf16[768,256]{1,0:T(8,128)(2,1)S(1)}, bf16[768,256]{1,0:T(8,128)(2,1)}) custom-call(f32[48,128]{1,0:T(8,128)S(1)} %copy-done.2, bf16[48,64,128]{2,1,0:T(8,128)(2,1)} %bitcast.18), custom_call_target="tpu_custom_call" | custom-call | bytes 1585152 | tf_op jit(solution)/shard_map/pallas_call | solution.py:649
  72.6 15.0 %all-to-all-done.2 = bf16[16,192,128]{2,1,0:T(8,128)(2,1)S(1)} async-done(((bf16[16,192,128]{2,1,0:T(8,128)(2,1)}), bf16[16,192,128]{2,1,0:T(8,128)(2,1)S(1)}, u32[]{:S(2)}, u32[]{:S(2)}) %all-to-all-start.2) | async-done | bytes 786464 | tf_op jit(solution)/shard_map/all_to_all | solution.py:673
  87.6 4.1 %shard_map.128 = (bf16[16,240,128]{2,1,0:T(8,128)(2,1)S(1)}, f32[512,128]{1,0:T(8,128)}) custom-call(bf16[48,64,128]{2,1,0:T(8,128)(2,1)S(1)} %bitcast.20, bf16[6272,48]{1,0:T(8,128)(2,1)S(1)} %shard_map.126.near_rows_ref, bf16[768,256]{1,0:T(8,128)(2,1)S(1)} %get-tuple-element.17.near_pairs_ref, bf16[512,128]{1,0:T(8,128)(2,1)S(1)} %copy-done.1, ...), custom_call_target="tpu_custom_call" | custom-call | flops 622854144 | bytes 29450754 | tf_op jit(solution)/shard_map/pallas_call | solution.py:649
  91.7 29.0 %all_to_all.25.received_ref = bf16[16,240,128]{2,1,0:T(8,128)(2,1)S(1)} all-to-all(bf16[16,240,128]{2,1,0:T(8,128)(2,1)S(1)} %get-tuple-element.20), channel_id=1, replica_groups=mesh['groups'=2,'space'=16] {'space'}, dimensions={0} | all-to-all | bytes 1966080 | tf_op jit(solution)/shard_map/all_to_all | solution.py:673
  120.7 0.7 shard_map.130
  121.4 4.7 %all-to-all-start.4 = ((bf16[16,48,128]{2,1,0:T(8,128)(2,1)}), bf16[16,48,128]{2,1,0:T(8,128)(2,1)S(1)}, u32[]{:S(2)}, u32[]{:S(2)}) async-start(bf16[16,48,128]{2,1,0:T(8,128)(2,1)} %shard_map.130), calls=%async_computation.4 | async-start | bytes 393216 | tf_op jit(solution)/shard_map/all_to_all | solution.py:673
  126.2 3.7 %shard_map.129 = bf16[3,1440,128]{2,1,0:T(8,128)(2,1)} custom-call(bf16[8,2,240,128]{3,2,1,0:T(8,128)(2,1)S(1)} %bitcast.16, bf16[3,1440,128]{2,1,0:T(8,128)(2,1)} %upstream_hbm.1, bf16[2,720,512]{2,1,0:T(8,128)(2,1)} %constant.28.clone.rows_hbm), custom_call_target="tpu_custom_call" | custom-call | flops 566231040 | bytes 4669440 | tf_op jit(solution)/shard_map/pallas_call | solution.py:649
  129.9 5.3 %all-to-all-done.4.received_ref = bf16[16,48,128]{2,1,0:T(8,128)(2,1)S(1)} async-done(((bf16[16,48,128]{2,1,0:T(8,128)(2,1)}), bf16[16,48,128]{2,1,0:T(8,128)(2,1)S(1)}, u32[]{:S(2)}, u32[]{:S(2)}) %all-to-all-start.4) | async-done | bytes 196640 | tf_op jit(solution)/shard_map/all_to_all | solution.py:673
  135.2 0.8 shard_map.131
  (4 shorter events, 0.0 us)
Async XLA Ops:
  4.2 26.1 %all-to-all-start = ((bf16[16,192,128]{2,1,0:T(8,128)(2,1)}), bf16[16,192,128]{2,1,0:T(8,128)(2,1)S(1)}, u32[]{:S(2)}, u32[]{:S(2)}) async-start(bf16[16,192,128]{2,1,0:T(8,128)(2,1)} %bitcast.22), calls=%async_computation | async-start | bytes 1572864 | tf_op jit(solution)/shard_map/all_to_all | solution.py:673
  11.6 18.7 %copy-start.1 = (bf16[512,128]{1,0:T(8,128)(2,1)S(1)}, bf16[512,128]{1,0:T(8,128)(2,1)}, u32[]{:S(2)}) copy-start(bf16[512,128]{1,0:T(8,128)(2,1)} %gain_ref.3) | copy-start | bytes 393220
  11.6 18.7 %copy-start.2 = (f32[48,128]{1,0:T(8,128)S(1)}, f32[48,128]{1,0:T(8,128)}, u32[]{:S(2)}) copy-start(f32[48,128]{1,0:T(8,128)} %constant.32.clone.weight_ref) | copy-start | bytes 73732
  30.3 3.6 %copy-start = (bf16[16,192,128]{2,1,0:T(8,128)(2,1)}, bf16[16,192,128]{2,1,0:T(8,128)(2,1)S(1)}, u32[]{:S(2)}) copy-start(bf16[16,192,128]{2,1,0:T(8,128)(2,1)S(1)} %all-to-all-done) | copy-start | bytes 2359300
  33.9 5.6 %copy-start.3 = (bf16[2,128,128]{2,1,0:T(8,128)(2,1)S(1)}, bf16[2,128,128]{2,1,0:T(8,128)(2,1)}, u32[]{:S(2)}) copy-start(bf16[2,128,128]{2,1,0:T(8,128)(2,1)} %param.12) | copy-start | bytes 196612
  34.0 24.3 %all-to-all-start.1 = ((bf16[16,192,128]{2,1,0:T(8,128)(2,1)}), bf16[16,192,128]{2,1,0:T(8,128)(2,1)S(1)}, u32[]{:S(2)}, u32[]{:S(2)}) async-start(bf16[16,192,128]{2,1,0:T(8,128)(2,1)} %bitcast.21), calls=%async_computation.1 | async-start | bytes 1572864 | tf_op jit(solution)/shard_map/all_to_all | solution.py:673
  63.4 24.2 %all-to-all-start.2 = ((bf16[16,192,128]{2,1,0:T(8,128)(2,1)}), bf16[16,192,128]{2,1,0:T(8,128)(2,1)S(1)}, u32[]{:S(2)}, u32[]{:S(2)}) async-start(bf16[16,192,128]{2,1,0:T(8,128)(2,1)} %bitcast.23), calls=%async_computation.2 | async-start | bytes 1572864 | tf_op jit(solution)/shard_map/all_to_all | solution.py:673
  121.4 13.7 %all-to-all-start.4 = ((bf16[16,48,128]{2,1,0:T(8,128)(2,1)}), bf16[16,48,128]{2,1,0:T(8,128)(2,1)S(1)}, u32[]{:S(2)}, u32[]{:S(2)}) async-start(bf16[16,48,128]{2,1,0:T(8,128)(2,1)} %shard_map.130), calls=%async_computation.4 | async-start | bytes 393216 | tf_op jit(solution)/shard_map/all_to_all | solution.py:673

commit v6 on v5

--- a/solution.py
+++ b/solution.py
@@ -13,7 +13,7 @@
 MODES = 512
 TABLE_BYTES = 64 * 1024 * 1024
 VMEM_BYTES = 18 * 1024 * 1024
-DELAY = 12
+DELAY = 20
 BF16 = jnp.bfloat16
 F32 = jnp.float32
 

time: 137 us -> 137 us (level)
  no operation moved by 1% of the time
where the time goes in v6:
time: 137 us; the launch traced here: 136 us
  waiting for transfers between devices  53.3 us (39%)
  blocking collectives  29 us (21%)
  Pallas kernels  27.6 us (20%)
  starting transfers between devices  23.2 us (17%)
  local copies, waits for them, and re-layouts  2.07 us (2%)
    all_to_all x4, waiting for transfers between devices, exchange(): lax.all_to_all(array, 'space', split_axis=0, concat_axis=0, tiled=True)  53.3 us
    all_to_all x1, blocking collectives, exchange(): lax.all_to_all(array, 'space', split_axis=0, concat_axis=0, tiled=True)  29 us
    pallas_call x11, Pallas kernels, call(): pl.pallas_call(kernel, out_shape=out_shape, in_specs=[pl.BlockSpec(memory...  27.6 us
    all_to_all x4, starting transfers between devices, exchange(): lax.all_to_all(array, 'space', split_axis=0, concat_axis=0, tiled=True)  23.2 us
  transfers between devices with their start and end apart: 4, of which 4 were waited for; matrix products, arithmetic and copies ran while one was open for 2% of the time, Pallas kernels for 7%

profile of v6, /device:TPU:0, one launch (start us, length us, event | category | flops | bytes accessed | tf_op | source)
XLA Modules:
  0.0 136.0 jit_solution(10470798043808530837)
XLA Ops:
  0.6 3.5 %shard_map.121 = bf16[8,2,192,128]{3,2,1,0:T(8,128)(2,1)} custom-call(bf16[3,1440,128]{2,1,0:T(8,128)(2,1)} %grid_hbm.1, bf16[2,512,720]{2,1,0:T(8,128)(2,1)} %constant.29.clone.columns_hbm), custom_call_target="tpu_custom_call" | custom-call | flops 566231040 | bytes 3366912 | tf_op jit(solution)/shard_map/pallas_call | solution.py:649
  4.2 7.4 %all-to-all-start = ((bf16[16,192,128]{2,1,0:T(8,128)(2,1)}), bf16[16,192,128]{2,1,0:T(8,128)(2,1)S(1)}, u32[]{:S(2)}, u32[]{:S(2)}) async-start(bf16[16,192,128]{2,1,0:T(8,128)(2,1)} %bitcast.22), calls=%async_computation | async-start | bytes 1572864 | tf_op jit(solution)/shard_map/all_to_all | solution.py:673
  11.6 0.0 copy-start.1
  11.6 0.0 copy-start.2
  11.6 1.7 %dynamic-slice_bitcast_fusion.rows_ref = bf16[8448,48]{1,0:T(8,128)(2,1)S(1)} fusion(bf16[16,8448,48]{2,1,0:T(8,128)(2,1)} %constant.30.clone.source_hbm.rows_hbm, s32[]{:T(128)S(6)} %select_n.8), kind=kLoop, calls=%fused_computation | loop fusion | bytes 1622020 | tf_op jit(solution)/shard_map/jit(dynamic_index_in_dim)/squeeze | solution.py:703
  13.3 17.0 %all-to-all-done = bf16[16,192,128]{2,1,0:T(8,128)(2,1)S(1)} async-done(((bf16[16,192,128]{2,1,0:T(8,128)(2,1)}), bf16[16,192,128]{2,1,0:T(8,128)(2,1)S(1)}, u32[]{:S(2)}, u32[]{:S(2)}) %all-to-all-start) | async-done | bytes 786464 | tf_op jit(solution)/shard_map/all_to_all | solution.py:673
  30.3 0.0 copy-start
  30.3 0.0 copy-done.1
  30.3 0.0 copy-done.2
  30.3 3.3 %shard_map.122 = bf16[48,64,128]{2,1,0:T(8,128)(2,1)} custom-call(bf16[48,64,128]{2,1,0:T(8,128)(2,1)S(1)} %bitcast.17, bf16[8448,48]{1,0:T(8,128)(2,1)S(1)} %dynamic-slice_bitcast_fusion.rows_ref, bf16[512,128]{1,0:T(8,128)(2,1)S(1)} %copy-done.1, f32[48,128]{1,0:T(8,128)S(1)} %copy-done.2, f32[1,256]{1,0:T(1,128)S(1)} %mul.3.alpha_ref, s32[1]{0:T(128)} %bitcast.place_ref, ...), custom_call_target="tpu_custom_call" | custom-call | flops 415236096 | bytes 15503874 | tf_op jit(solution)/shard_map/pallas_call | solution.py:649
  33.7 0.0 copy-done
  33.7 0.0 copy-start.3
  33.7 5.6 %all-to-all-start.1 = ((bf16[16,192,128]{2,1,0:T(8,128)(2,1)}), bf16[16,192,128]{2,1,0:T(8,128)(2,1)S(1)}, u32[]{:S(2)}, u32[]{:S(2)}) async-start(bf16[16,192,128]{2,1,0:T(8,128)(2,1)} %bitcast.21), calls=%async_computation.1 | async-start | bytes 1572864 | tf_op jit(solution)/shard_map/all_to_all | solution.py:673
  39.3 0.0 copy-done.3
  39.3 0.1 copy.17
  39.4 0.1 copy.16
  39.6 0.1 copy.15.wide_ref
  39.7 1.3 shard_map.123.upstream_ref
  41.0 1.0 shard_map.124.first_ref
  42.0 16.0 %all-to-all-done.1 = bf16[16,192,128]{2,1,0:T(8,128)(2,1)S(1)} async-done(((bf16[16,192,128]{2,1,0:T(8,128)(2,1)}), bf16[16,192,128]{2,1,0:T(8,128)(2,1)S(1)}, u32[]{:S(2)}, u32[]{:S(2)}) %all-to-all-start.1) | async-done | bytes 786464 | tf_op jit(solution)/shard_map/all_to_all | solution.py:673
  58.0 5.1 %shard_map.125 = (bf16[8,2,192,128]{3,2,1,0:T(8,128)(2,1)}, f32[256,128]{1,0:T(8,128)S(1)}) custom-call(bf16[8,2,192,128]{3,2,1,0:T(8,128)(2,1)S(1)} %bitcast.19, bf16[256,256]{1,0:T(8,128)(2,1)S(1)} %copy.15.wide_ref, bf16[256,256]{1,0:T(8,128)(2,1)S(1)} %get-tuple-element.23.wide_t_ref, bf16[3,1440,128]{2,1,0:T(8,128)(2,1)S(1)} %shard_map.123.upstream_ref, ...), custom_call_target="tpu_custom_call" | custom-call | flops 1132462080 | bytes 6447104 | tf_op jit(solution)/shard_map/pallas_call | solution.py:649
  63.1 5.5 %all-to-all-start.2 = ((bf16[16,192,128]{2,1,0:T(8,128)(2,1)}), bf16[16,192,128]{2,1,0:T(8,128)(2,1)S(1)}, u32[]{:S(2)}, u32[]{:S(2)}) async-start(bf16[16,192,128]{2,1,0:T(8,128)(2,1)} %bitcast.23), calls=%async_computation.2 | async-start | bytes 1572864 | tf_op jit(solution)/shard_map/all_to_all | solution.py:673
  68.6 1.4 %shard_map.126.near_rows_ref = bf16[6272,48]{1,0:T(8,128)(2,1)S(1)} custom-call(s32[1]{0:T(128)} %bitcast.place_ref, bf16[16,8448,48]{2,1,0:T(8,128)(2,1)} %constant.30.clone.source_hbm.rows_hbm), custom_call_target="tpu_custom_call" | custom-call | bytes 13578242 | tf_op jit(solution)/shard_map/pallas_call | solution.py:649
  70.1 2.2 %shard_map.127 = (bf16[768,256]{1,0:T(8,128)(2,1)S(1)}, bf16[768,256]{1,0:T(8,128)(2,1)}) custom-call(f32[48,128]{1,0:T(8,128)S(1)} %copy-done.2, bf16[48,64,128]{2,1,0:T(8,128)(2,1)} %bitcast.18), custom_call_target="tpu_custom_call" | custom-call | bytes 1585152 | tf_op jit(solution)/shard_map/pallas_call | solution.py:649
  72.3 15.0 %all-to-all-done.2 = bf16[16,192,128]{2,1,0:T(8,128)(2,1)S(1)} async-done(((bf16[16,192,128]{2,1,0:T(8,128)(2,1)}), bf16[16,192,128]{2,1,0:T(8,128)(2,1)S(1)}, u32[]{:S(2)}, u32[]{:S(2)}) %all-to-all-start.2) | async-done | bytes 786464 | tf_op jit(solution)/shard_map/all_to_all | solution.py:673
  87.3 4.4 %shard_map.128 = (bf16[16,240,128]{2,1,0:T(8,128)(2,1)S(1)}, f32[512,128]{1,0:T(8,128)}) custom-call(bf16[48,64,128]{2,1,0:T(8,128)(2,1)S(1)} %bitcast.20, bf16[6272,48]{1,0:T(8,128)(2,1)S(1)} %shard_map.126.near_rows_ref, bf16[768,256]{1,0:T(8,128)(2,1)S(1)} %get-tuple-element.17.near_pairs_ref, bf16[512,128]{1,0:T(8,128)(2,1)S(1)} %copy-done.1, ...), custom_call_target="tpu_custom_call" | custom-call | flops 622854144 | bytes 29450754 | tf_op jit(solution)/shard_map/pallas_call | solution.py:649
  91.8 29.0 %all_to_all.25.received_ref = bf16[16,240,128]{2,1,0:T(8,128)(2,1)S(1)} all-to-all(bf16[16,240,128]{2,1,0:T(8,128)(2,1)S(1)} %get-tuple-element.20), channel_id=1, replica_groups=mesh['groups'=2,'space'=16] {'space'}, dimensions={0} | all-to-all | bytes 1966080 | tf_op jit(solution)/shard_map/all_to_all | solution.py:673
  120.8 0.7 shard_map.130
  121.5 4.7 %all-to-all-start.4 = ((bf16[16,48,128]{2,1,0:T(8,128)(2,1)}), bf16[16,48,128]{2,1,0:T(8,128)(2,1)S(1)}, u32[]{:S(2)}, u32[]{:S(2)}) async-start(bf16[16,48,128]{2,1,0:T(8,128)(2,1)} %shard_map.130), calls=%async_computation.4 | async-start | bytes 393216 | tf_op jit(solution)/shard_map/all_to_all | solution.py:673
  126.2 3.7 %shard_map.129 = bf16[3,1440,128]{2,1,0:T(8,128)(2,1)} custom-call(bf16[8,2,240,128]{3,2,1,0:T(8,128)(2,1)S(1)} %bitcast.16, bf16[3,1440,128]{2,1,0:T(8,128)(2,1)} %upstream_hbm.1, bf16[2,720,512]{2,1,0:T(8,128)(2,1)} %constant.28.clone.rows_hbm), custom_call_target="tpu_custom_call" | custom-call | flops 566231040 | bytes 4669440 | tf_op jit(solution)/shard_map/pallas_call | solution.py:649
  129.9 5.3 %all-to-all-done.4.received_ref = bf16[16,48,128]{2,1,0:T(8,128)(2,1)S(1)} async-done(((bf16[16,48,128]{2,1,0:T(8,128)(2,1)}), bf16[16,48,128]{2,1,0:T(8,128)(2,1)S(1)}, u32[]{:S(2)}, u32[]{:S(2)}) %all-to-all-start.4) | async-done | bytes 196640 | tf_op jit(solution)/shard_map/all_to_all | solution.py:673
  135.2 0.8 shard_map.131
  (4 shorter events, 0.0 us)
Async XLA Ops:
  4.2 26.1 %all-to-all-start = ((bf16[16,192,128]{2,1,0:T(8,128)(2,1)}), bf16[16,192,128]{2,1,0:T(8,128)(2,1)S(1)}, u32[]{:S(2)}, u32[]{:S(2)}) async-start(bf16[16,192,128]{2,1,0:T(8,128)(2,1)} %bitcast.22), calls=%async_computation | async-start | bytes 1572864 | tf_op jit(solution)/shard_map/all_to_all | solution.py:673
  11.6 18.7 %copy-start.1 = (bf16[512,128]{1,0:T(8,128)(2,1)S(1)}, bf16[512,128]{1,0:T(8,128)(2,1)}, u32[]{:S(2)}) copy-start(bf16[512,128]{1,0:T(8,128)(2,1)} %gain_ref.3) | copy-start | bytes 393220
  11.6 18.7 %copy-start.2 = (f32[48,128]{1,0:T(8,128)S(1)}, f32[48,128]{1,0:T(8,128)}, u32[]{:S(2)}) copy-start(f32[48,128]{1,0:T(8,128)} %constant.32.clone.weight_ref) | copy-start | bytes 73732
  30.3 3.4 %copy-start = (bf16[16,192,128]{2,1,0:T(8,128)(2,1)}, bf16[16,192,128]{2,1,0:T(8,128)(2,1)S(1)}, u32[]{:S(2)}) copy-start(bf16[16,192,128]{2,1,0:T(8,128)(2,1)S(1)} %all-to-all-done) | copy-start | bytes 2359300
  33.7 5.6 %copy-start.3 = (bf16[2,128,128]{2,1,0:T(8,128)(2,1)S(1)}, bf16[2,128,128]{2,1,0:T(8,128)(2,1)}, u32[]{:S(2)}) copy-start(bf16[2,128,128]{2,1,0:T(8,128)(2,1)} %param.12) | copy-start | bytes 196612
  33.7 24.3 %all-to-all-start.1 = ((bf16[16,192,128]{2,1,0:T(8,128)(2,1)}), bf16[16,192,128]{2,1,0:T(8,128)(2,1)S(1)}, u32[]{:S(2)}, u32[]{:S(2)}) async-start(bf16[16,192,128]{2,1,0:T(8,128)(2,1)} %bitcast.21), calls=%async_computation.1 | async-start | bytes 1572864 | tf_op jit(solution)/shard_map/all_to_all | solution.py:673
  63.1 24.2 %all-to-all-start.2 = ((bf16[16,192,128]{2,1,0:T(8,128)(2,1)}), bf16[16,192,128]{2,1,0:T(8,128)(2,1)S(1)}, u32[]{:S(2)}, u32[]{:S(2)}) async-start(bf16[16,192,128]{2,1,0:T(8,128)(2,1)} %bitcast.23), calls=%async_computation.2 | async-start | bytes 1572864 | tf_op jit(solution)/shard_map/all_to_all | solution.py:673
  121.5 13.7 %all-to-all-start.4 = ((bf16[16,48,128]{2,1,0:T(8,128)(2,1)}), bf16[16,48,128]{2,1,0:T(8,128)(2,1)S(1)}, u32[]{:S(2)}, u32[]{:S(2)}) async-start(bf16[16,48,128]{2,1,0:T(8,128)(2,1)} %shard_map.130), calls=%async_computation.4 | async-start | bytes 393216 | tf_op jit(solution)/shard_map/all_to_all | solution.py:673
